TPU v7x, 128 devices: a whole 4x4x4 slice. The times are simulated.
128 devices in a mesh: dp: 16 (over x, z), ctx: 8 (over y, core).
Axes of the slice: x: 4, y: 4, z: 4, core: 2. Of those that a mesh axis runs over, the one named last changes fastest.
Arguments:
- tokens: bfloat16 [64, 5120, 1280], P('dp', 'ctx'), may hold values from -64 to 64
- router: bfloat16 [1280, 256], replicated, may hold values from -1 to 1
- expert_up: bfloat16 [128, 1280, 2560], P(('dp', 'ctx')), may hold values from -0.5 to 0.5
- expert_down: bfloat16 [128, 2560, 1280], P(('dp', 'ctx')), may hold values from -0.25 to 0.25
Outputs:
- mixed: bfloat16 [64, 5120, 1280], P('dp', 'ctx')
All inputs are finite; a program needn't handle non-finite values.
Results may differ from a plain program's by a relative error of at most 0.015.
Values may be sent and summed in bfloat16 or wider, within the bound.
No kernel may reach another device: no remote copies, remote signals or barrier semaphores. Data moves between devices by JAX's collectives and lax.ppermute only.
A program may use at most 128 MiB of HBM per device.

v0:
```python
import jax
import jax.numpy as jnp
from jax import lax
from jax.sharding import PartitionSpec as P


def expert_rows(grouped, up_matrix, down_matrix):
    feature = grouped.shape[-1]
    flat = grouped.reshape(-1, feature)
    hidden = jax.nn.gelu(
        jnp.dot(flat, up_matrix, preferred_element_type=jnp.float32), approximate=False
    ).astype(jnp.bfloat16)
    produced = jnp.dot(hidden, down_matrix, preferred_element_type=jnp.float32).astype(jnp.bfloat16)
    return produced.reshape(grouped.shape)


def shards(tokens, router, expert_up, expert_down):
    clip_dev, tok_dev, feature = tokens.shape
    dp_size = lax.axis_size("dp")
    ctx_size = lax.axis_size("ctx")
    slot_total = router.shape[1]
    per_expert = slot_total // (dp_size * ctx_size)
    ordered = (
        router.reshape(feature, dp_size, ctx_size, per_expert)
        .transpose(0, 2, 1, 3)
        .reshape(feature, slot_total)
    )
    logits = jnp.einsum("ctd,dj->ctj", tokens, ordered, preferred_element_type=jnp.float32)
    local_max = jnp.max(logits, axis=1)
    column_max = lax.pmax(local_max, "ctx")
    exponent = jnp.exp(logits - column_max[:, None, :])
    column_sum = lax.psum(jnp.sum(exponent, axis=1), "ctx")
    dispatch = (exponent / column_sum[:, None, :]).astype(jnp.bfloat16)
    row_max = jnp.max(logits, axis=2)
    row_exp = jnp.exp(logits - row_max[:, :, None])
    combine = (row_exp / jnp.sum(row_exp, axis=2)[:, :, None]).astype(jnp.bfloat16)
    up_matrix = expert_up[0]
    down_matrix = expert_down[0]
    split_dispatch = dispatch.reshape(clip_dev, tok_dev, ctx_size, dp_size, per_expert)
    partial_value = jnp.einsum(
        "ctabs,ctd->cbasd", split_dispatch, tokens, preferred_element_type=jnp.float32
    ).astype(jnp.bfloat16)
    grouped = partial_value.reshape(clip_dev, dp_size * ctx_size, per_expert, feature)
    received = lax.all_to_all(grouped, ("dp", "ctx"), split_axis=1, concat_axis=1, tiled=True)
    amount = received.shape[0]
    blocks = received.astype(jnp.float32).reshape(amount, dp_size, ctx_size, per_expert, feature)
    results = expert_rows(jnp.sum(blocks, axis=2).astype(jnp.bfloat16), up_matrix, down_matrix)
    returned = lax.all_to_all(results, "dp", split_axis=1, concat_axis=1, tiled=True)
    returned = returned.reshape(clip_dev, dp_size * per_expert, feature)
    mixed = jnp.einsum(
        "ctj,cjd->ctd",
        combine,
        lax.all_gather(returned, "ctx", axis=1, tiled=True),
        preferred_element_type=jnp.float32,
    )
    return mixed.astype(jnp.bfloat16)


def solution(mesh):
    in_specs = (
        P("dp", "ctx", None),
        P(),
        P(("dp", "ctx"), None, None),
        P(("dp", "ctx"), None, None),
    )
    out_specs = P("dp", "ctx", None)
    return jax.shard_map(shards, mesh=mesh, in_specs=in_specs, out_specs=out_specs, check_vma=False)
```

profile of v0, /device:TPU:1, one launch (start us, length us, event | category | flops | bytes accessed | tf_op | source)
XLA Modules:
  0.0 165.4 jit_solution(12961992208688201916)
XLA Ops:
  6.5 0.0 all-gather.2.cloned.1.call-start
  6.5 1.3 copy.26
  7.9 0.2 reshape.37
  8.1 0.5 copy.27
  8.6 0.2 reshape.45
  8.8 4.8 %fusion.94 = (f32[4,256]{1,0:T(4,128)S(1)}, f32[4,640,256]{1,2,0:T(8,128)S(1)}) fusion(bf16[4,640,1280]{2,1,0:T(8,128)(2,1)} %param.4, bf16[1280,256,1]{0,1,2:T(8,128)(2,1)S(1)} %reshape.45), kind=kOutput, calls=%fused_computation.100 | convolution fusion | flops 1678375936 | bytes 9834496 | tf_op jit(solution)/shard_map/ctd,dj->ctj/dot_general | solution.py:28
  13.7 13.5 %pmax.7 = f32[4,256]{1,0:T(4,128)S(1)} all-reduce(f32[4,256]{1,0:T(4,128)S(1)} %get-tuple-element.5), channel_id=1, replica_groups=mesh['dp'=16,'ctx'=8] {'ctx'}, use_global_device_ids=true, to_apply=%region_3.0 | all-reduce | flops 1024 | bytes 8192 | tf_op jit(solution)/shard_map/pmax | solution.py:30
  27.1 0.9 fusion.16
  28.0 14.7 %psum.7 = f32[4,256]{1,0:T(4,128)S(1)} all-reduce(f32[4,256]{1,0:T(4,128)S(1)} %fusion.16), channel_id=1, replica_groups=mesh['dp'=16,'ctx'=8] {'ctx'}, use_global_device_ids=true, to_apply=%region_5.0 | all-reduce | flops 1024 | bytes 8192 | tf_op jit(solution)/shard_map/psum | solution.py:32
  42.7 1.6 divide_convert_fusion
  44.3 4.0 %reshape.39 = bf16[4,640,8,16,2]{1,4,3,2,0:T(2,128)(2,1)} reshape(bf16[4,640,256]{1,2,0:T(8,128)(2,1)} %divide_convert_fusion) | data formatting | bytes 2621440 | tf_op jit(solution)/shard_map/reshape | solution.py:39
  48.2 5.5 %fusion.10 = bf16[4,16,8,2,1280]{4,1,3,2,0:T(8,128)(2,1)S(1)} fusion(bf16[4,640,1280]{2,1,0:T(8,128)(2,1)} %param.4, bf16[4,640,8,16,2]{1,4,3,2,0:T(2,128)(2,1)} %reshape.39), kind=kOutput, calls=%fused_computation.9 | convolution fusion | flops 1679032320 | bytes 10485760 | tf_op jit(solution)/shard_map/ctabs,ctd->cbasd/dot_general | solution.py:40
  53.7 1.4 copy.43
  55.2 2.7 %copy.30 = bf16[4,128,2,1280]{3,2,0,1:T(2,128)(2,1)S(1)} copy(bf16[4,128,2,1280]{3,1,2,0:T(8,128)(2,1)S(1)} %bitcast.41) | data formatting | bytes 5242880 | tf_op jit(solution)/shard_map/reshape | solution.py:43
  57.9 43.9 %all_to_all.10 = bf16[4,128,2,1280]{3,2,0,1:T(2,128)(2,1)S(1)} all-to-all(bf16[4,128,2,1280]{3,2,0,1:T(2,128)(2,1)S(1)} %copy.30), channel_id=1, replica_groups=mesh['dp'=16,'ctx'=8] {'dp','ctx'}, dimensions={1} | all-to-all | bytes 5242880 | tf_op jit(solution)/shard_map/all_to_all | solution.py:44
  101.8 2.3 %bitcast_reduce_fusion = bf16[4,16,2,1280]{3,2,0,1:T(2,128)(2,1)S(1)} fusion(bf16[4,128,2,1280]{3,2,0,1:T(2,128)(2,1)S(1)} %all_to_all.10), kind=kLoop, calls=%fused_computation.10 | loop fusion | flops 1146880 | bytes 2949120 | tf_op jit(solution)/shard_map/reduce_sum | solution.py:47
  104.0 0.2 copy.32
  104.3 0.1 convert_element_type.40
  104.4 10.0 %fusion.13 = bf16[128,1280]{1,0:T(8,128)(2,1)} fusion(bf16[1,2560,1280]{2,1,0:T(8,128)(2,1)} %param.7, bf16[128,1280]{1,0:T(8,128)(2,1)S(1)} %convert_element_type.40, bf16[1,1280,2560]{2,1,0:T(8,128)(2,1)} %param.6), kind=kOutput, calls=%fused_computation.16 | convolution fusion | flops 1699184640 | bytes 13762560 | tf_op jit(solution)/shard_map/dot_general | solution.py:13
  114.4 1.1 reshape.43
  115.5 0.2 copy.33
  115.7 10.4 %all_to_all.11 = bf16[4,16,2,1280]{3,2,0,1:T(2,128)(2,1)S(1)} all-to-all(bf16[4,16,2,1280]{3,2,0,1:T(2,128)(2,1)S(1)} %copy.33), channel_id=1, replica_groups=mesh['dp'=16,'ctx'=8] {'dp'}, dimensions={1} | all-to-all | bytes 655360 | tf_op jit(solution)/shard_map/all_to_all | solution.py:48
  126.1 0.2 copy.34
  126.3 0.8 reshape.44
  127.2 0.0 all-gather.2.cloned.1.call-update
  127.2 0.5 fusion.95
  127.7 24.3 %all-gather.2.cloned.1.call-done = bf16[4,256,1280]{2,1,0:T(8,128)(2,1)} async-done(((bf16[4,32,1280]{2,1,0:T(8,128)(2,1)}), bf16[4,256,1280]{2,1,0:T(8,128)(2,1)}) %all-gather.2.cloned.1.call-update) | async-done | bytes 2621456 | tf_op jit(solution)/shard_map/all_gather | solution.py:53
  152.0 6.5 %convolution_convert_fusion = bf16[4,640,1280]{2,1,0:T(8,128)(2,1)} fusion(bf16[4,256,1280]{2,1,0:T(8,128)(2,1)} %all-gather.2.cloned.1.call-done, f32[4,640]{1,0:T(4,128)S(1)} %fusion.95, f32[4,640,256]{1,2,0:T(8,128)S(1)} %get-tuple-element.6), kind=kOutput, calls=%fused_computation.7 | convolution fusion | flops 1682967296 | bytes 11806720 | tf_op jit(solution)/shard_map/ctj,cjd->ctd/dot_general | solution.py:50
Async XLA Ops:
  6.5 145.5 %all-gather.2.cloned.1.call-start = ((), (), s32[]{:S(2)}) async-start(), calls=%async_computation.2 | async-start | bytes 2949120 | tf_op jit(solution)/shard_map/all_gather | solution.py:53
Sparse Core Ops, SparseCore 0:
  127.3 24.6 all-gather.1
where the time goes:
time: 166 us; the launch traced here: 165 us
  blocking collectives  82.4 us (50%)
  matrix products  26.8 us (16%)
  waiting for transfers between devices  24.3 us (15%)
  between operations  13.5 us (8%)
  local copies, waits for them, and re-layouts  13.1 us (8%)
  other arithmetic  5.2 us (3%)
    all_to_all x1, blocking collectives, shards(): lax.all_to_all(grouped, ('dp', 'ctx'), split_axis=1, concat_axis=1, tiled...  43.9 us
    all_gather x1, waiting for transfers between devices, shards(): lax.all_gather(returned, 'ctx', axis=1, tiled=True)  24.3 us
    psum x1, blocking collectives, shards(): column_sum = lax.psum(jnp.sum(exponent, axis=1), 'ctx')  14.7 us
    pmax x1, blocking collectives, shards(): column_max = lax.pmax(local_max, 'ctx')  13.5 us
    all_to_all x1, blocking collectives, shards(): lax.all_to_all(results, 'dp', split_axis=1, concat_axis=1, tiled=True)  10.4 us
    dot_general x1, matrix products, expert_rows(): jnp.dot(hidden, down_matrix, preferred_element_type=jnp.float32)  9.99 us
    dot_general x1, matrix products, shards(): jnp.einsum('ctj,cjd->ctd', combine, lax.all_gather(returned, 'ctx', axis=...  6.49 us
    dot_general x1, matrix products, shards(): jnp.einsum('ctabs,ctd->cbasd', split_dispatch, tokens, preferred_element_...  5.47 us
  transfers between devices with their start and end apart: 1, of which 1 were waited for; matrix products, arithmetic and copies ran while one was open for 0% of the time, Pallas kernels for 0%

commit v1 on v0

v1 whole, which is shorter than its diff:
```python
import functools

import jax
import jax.numpy as jnp
import numpy as np
from jax import lax
from jax.experimental import pallas as pl
from jax.experimental.pallas import tpu as pltpu
from jax.sharding import Mesh
from jax.sharding import PartitionSpec as P

F32, BF16 = jnp.float32, jnp.bfloat16
STAT = 128
CHIPS, PLACES, LINE, CORES = 64, 16, 4, 2
MIB = 1024 * 1024


def iota(shape, dim):
    return lax.broadcasted_iota(jnp.int32, shape, dim)


def pieces(value, count):
    out = []
    for _ in range(count):
        part = value.astype(BF16).astype(F32)
        out.append(part)
        value = value - part
    return out


def read_stats(stats):
    return stats[:, 0:1] + stats[:, 1:2] + stats[:, 2:3], stats[:, 3:4] + stats[:, 4:5]


def interleave(rows, back):
    new = iota((rows, rows), 1 if back else 0)
    old = iota((rows, rows), 0 if back else 1)
    place = (new // 2) % 4 * 32 + new // 8 * 2 + new % 2
    return jnp.where(old == place, 1.0, 0.0).astype(BF16)


def dispatch_kernel(core_ref, tokens_ref, router_ref, mine_ref, other_ref, logits_ref, ordered_ref):
    slots = router_ref.shape[1]
    half = slots // CORES

    @pl.when(pl.program_id(0) == 0)
    def _():
        row, column = iota((slots, slots), 0), iota((slots, slots), 1)
        core = core_ref[0]
        owner = jnp.where(column < half, core, 1 - core)
        within = column % half
        source = within // 2 * 4 + owner * 2 + within % 2
        chosen = jnp.where(row == source, 1.0, 0.0).astype(BF16)
        ordered_ref[...] = jnp.dot(router_ref[...], chosen, preferred_element_type=F32).astype(BF16)

    tokens = tokens_ref[0]
    logits = jnp.dot(tokens, ordered_ref[...], preferred_element_type=F32)
    logits_ref[0] = logits
    top = jnp.max(logits, axis=0, keepdims=True)
    exponent = jnp.exp(logits - top)
    total = jnp.sum(exponent, axis=0, keepdims=True)
    rows = pieces(top, 3) + pieces(total, 2) + [1.0 / total]
    rows.append(jnp.zeros((STAT - len(rows), slots), F32))
    stats = jnp.concatenate(rows, axis=0).T
    sums = lax.dot_general(exponent.astype(BF16), tokens, (((0,), (0,)), ((), ())), preferred_element_type=F32)
    sums = (sums * stats[:, 5:6]).astype(BF16)
    stats = stats.astype(BF16)
    depth = tokens.shape[1]
    mine_ref[0, :, :depth] = sums[:half]
    mine_ref[0, :, depth:] = stats[:half]
    other_ref[0, :, :depth] = sums[half:]
    other_ref[0, :, depth:] = stats[half:]


def combine_kernel(logits_ref, combine_ref):
    logits = logits_ref[0]
    exponent = jnp.exp(logits - jnp.max(logits, axis=1, keepdims=True))
    combine_ref[0] = (exponent / jnp.sum(exponent, axis=1, keepdims=True)).astype(BF16)


def merge_kernel(mine_ref, theirs_ref, out_ref):
    clips, part, width = mine_ref.shape
    depth = width - STAT
    rows = clips * part
    a = mine_ref[...].astype(F32).reshape(rows, width)
    b = theirs_ref[...].astype(F32).reshape(rows, width)
    top_a, total_a = read_stats(a[:, depth:])
    top_b, total_b = read_stats(b[:, depth:])
    top = jnp.maximum(top_a, top_b)
    weight_a = total_a * jnp.exp(top_a - top)
    weight_b = total_b * jnp.exp(top_b - top)
    total = weight_a + weight_b
    inverse = 1.0 / total
    sums = a[:, :depth] * (weight_a * inverse) + b[:, :depth] * (weight_b * inverse)
    lane = iota((rows, STAT), 1)
    stats = jnp.zeros((rows, STAT), F32)
    for k, value in enumerate(pieces(top, 3) + pieces(total, 2)):
        stats = jnp.where(lane == k, value, stats)
    order = interleave(rows, False)
    for lo, hi, value in ((0, depth, sums), (depth, width, stats)):
        moved = jnp.dot(order, value.astype(BF16), preferred_element_type=F32)
        out_ref[:, :, lo:hi] = moved.reshape(out_ref.shape[0], out_ref.shape[1], hi - lo).astype(BF16)


def expert_kernel(tile, received_ref, up_ref, down_ref, out_ref, rows_ref):
    depth = up_ref.shape[1]
    for place in range(PLACES):
        parts = [received_ref[place * LINE + y].astype(F32) for y in range(LINE)]
        stats = [read_stats(part[:, depth:]) for part in parts]
        top = functools.reduce(jnp.maximum, [s[0] for s in stats])
        weights = [s[1] * jnp.exp(s[0] - top) for s in stats]
        inverse = 1.0 / sum(weights)
        rows_ref[place * 8:place * 8 + 8, :] = sum(
            part[:, :depth] * (weight * inverse) for part, weight in zip(parts, weights)
        )
    rows = rows_ref[...].astype(BF16)
    result = jnp.zeros(rows.shape, F32)
    for start in range(0, up_ref.shape[2], tile):
        hidden = jnp.dot(rows, up_ref[0, :, start:start + tile], preferred_element_type=F32)
        hidden = (0.5 * hidden * (1.0 + lax.erf(hidden * np.float32(np.sqrt(0.5))))).astype(BF16)
        result = result + jnp.dot(hidden, down_ref[0, start:start + tile, :], preferred_element_type=F32)
    result = result.reshape(PLACES, 8, depth).astype(BF16)
    for place in range(PLACES):
        for y in range(LINE):
            out_ref[place * LINE + y] = result[place]


def mix_kernel(mine_ref, theirs_ref, combine_ref, out_ref, slots_ref):
    clips = slots_ref.shape[0]
    half = slots_ref.shape[1] // CORES
    depth = slots_ref.shape[2]

    @pl.when(pl.program_id(0) == 0)
    def _():
        order = interleave(128, True)
        for core, ref in enumerate((mine_ref, theirs_ref)):
            for group in range(CHIPS // 16):
                block = ref[group * 16:group * 16 + 16].astype(F32).reshape(128, depth).astype(BF16)
                moved = jnp.dot(order, block, preferred_element_type=F32).astype(BF16)
                for clip in range(clips):
                    at = core * half + group * 32
                    slots_ref[clip, at:at + 32, :] = moved[clip * 32:clip * 32 + 32]

    slots = slots_ref[pl.program_id(0)]
    out_ref[0] = jnp.dot(combine_ref[0], slots, preferred_element_type=F32).astype(BF16)


def params(mib):
    return pltpu.CompilerParams(vmem_limit_bytes=mib * MIB)


def shards(tokens, router, expert_up, expert_down):
    clips, count, depth = tokens.shape
    slots = router.shape[1]
    half = slots // CORES
    wide = depth + STAT
    hidden = expert_up.shape[2]
    core = lax.axis_index("core").astype(jnp.int32).reshape(1)
    swap = [(0, 1), (1, 0)]
    chips = ("x", "z", "y")

    mine, other, logits = pl.pallas_call(
        dispatch_kernel,
        grid=(clips,),
        in_specs=[
            pl.BlockSpec(memory_space=pltpu.SMEM),
            pl.BlockSpec((1, count, depth), lambda c: (c, 0, 0)),
            pl.BlockSpec((depth, slots), lambda c: (0, 0)),
        ],
        out_specs=[
            pl.BlockSpec((1, half, wide), lambda c: (c, 0, 0)),
            pl.BlockSpec((1, half, wide), lambda c: (c, 0, 0)),
            pl.BlockSpec((1, count, slots), lambda c: (c, 0, 0)),
        ],
        out_shape=[
            jax.ShapeDtypeStruct((clips, half, wide), BF16),
            jax.ShapeDtypeStruct((clips, half, wide), BF16),
            jax.ShapeDtypeStruct((clips, count, slots), F32),
        ],
        scratch_shapes=[pltpu.VMEM((depth, slots), BF16)],
        compiler_params=params(24),
    )(core, tokens, router)

    theirs = lax.ppermute(other, "core", swap)

    merged = pl.pallas_call(
        merge_kernel,
        grid=(CHIPS // 16,),
        in_specs=[pl.BlockSpec((clips, 32, wide), lambda g: (0, g, 0))] * 2,
        out_specs=pl.BlockSpec((16, 8, wide), lambda g: (g, 0, 0)),
        out_shape=jax.ShapeDtypeStruct((CHIPS, 8, wide), BF16),
        compiler_params=params(16),
    )(mine, theirs)

    received = lax.all_to_all(merged, chips, 0, 0, tiled=False)

    combine = pl.pallas_call(
        combine_kernel,
        grid=(clips,),
        in_specs=[pl.BlockSpec((1, count, slots), lambda c: (c, 0, 0))],
        out_specs=pl.BlockSpec((1, count, slots), lambda c: (c, 0, 0)),
        out_shape=jax.ShapeDtypeStruct((clips, count, slots), BF16),
        compiler_params=params(12),
    )(logits)

    whole = pl.BlockSpec(memory_space=pltpu.VMEM)
    results = pl.pallas_call(
        functools.partial(expert_kernel, 512),
        in_specs=[whole] * 3,
        out_specs=whole,
        out_shape=jax.ShapeDtypeStruct((CHIPS, 8, depth), BF16),
        scratch_shapes=[pltpu.VMEM((PLACES * 8, depth), F32)],
        compiler_params=params(32),
    )(received, expert_up, expert_down)

    returned = lax.all_to_all(results, chips, 0, 0, tiled=False)
    partner = lax.ppermute(returned, "core", swap)

    full = pl.BlockSpec((CHIPS, 8, depth), lambda c: (0, 0, 0))
    return pl.pallas_call(
        mix_kernel,
        grid=(clips,),
        in_specs=[full, full, pl.BlockSpec((1, count, slots), lambda c: (c, 0, 0))],
        out_specs=pl.BlockSpec((1, count, depth), lambda c: (c, 0, 0)),
        out_shape=jax.ShapeDtypeStruct((clips, count, depth), BF16),
        scratch_shapes=[pltpu.VMEM((clips, slots, depth), BF16)],
        compiler_params=params(32),
    )(returned, partner, combine)


def solution(mesh):
    fine = Mesh(np.asarray(mesh.devices).reshape(4, 4, LINE, CORES), ("x", "z", "y", "core"))
    in_specs = (
        P(("x", "z"), ("y", "core"), None),
        P(),
        P(("x", "z", "y", "core"), None, None),
        P(("x", "z", "y", "core"), None, None),
    )
    out_specs = P(("x", "z"), ("y", "core"), None)
    return jax.shard_map(shards, mesh=fine, in_specs=in_specs, out_specs=out_specs, check_vma=False)
```

time: 166 us -> 91 us (0.55)
  matrix products: 26.8 us -> 0 us
  blocking collectives: 82.4 us -> 56 us
  Pallas kernels: 0 us -> 20.9 us
  waiting for transfers between devices: 24.3 us -> 4.46 us
  between operations: 13.5 us -> 0.04 us
  local copies, waits for them, and re-layouts: 13.1 us -> 3.95 us
  starting transfers between devices: 0.01 us -> 5.47 us
  other arithmetic: 5.2 us -> 0 us
    dot_general x4 -> x0, matrix products: 26.8 us -> none  [the longest x1 9.99 us: expert_rows(): jnp.dot(hidden, down_matrix, preferred_element_type=jnp.float32)]
    all_gather x1 -> x0, waiting for transfers between devices: 24.3 us -> none  [shards(): lax.all_gather(returned, 'ctx', axis=1, tiled=True)]
    pallas_call x0 -> x5, Pallas kernels: none -> 20.9 us  [the longest x1 9.36 us: shards(): pl.pallas_call(dispatch_kernel, grid=(clips,), in_specs=[pl.BlockSpec(mem...]
    psum x1 -> x0, blocking collectives: 14.7 us -> none  [shards(): column_sum = lax.psum(jnp.sum(exponent, axis=1), 'ctx')]
    pmax x1 -> x0, blocking collectives: 13.5 us -> none  [shards(): column_max = lax.pmax(local_max, 'ctx')]
    reshape x7 -> x0, local copies, waits for them, and re-layouts: 9.33 us -> none  [the longest x1 3.96 us: shards(): dispatch.reshape(clip_dev, tok_dev, ctx_size, dp_size, per_expert)]
    ppermute x0 -> x2, starting transfers between devices: none -> 5.47 us  [the longest x1 3.96 us: shards(): partner = lax.ppermute(returned, 'core', swap)]
    ppermute x0 -> x2, waiting for transfers between devices: none -> 4.46 us  [the longest x1 2.85 us: shards(): theirs = lax.ppermute(other, 'core', swap)]
  transfers between devices with their start and end apart: 1 -> 2, of which waited for: 1 -> 2; matrix products, arithmetic and copies ran while one was open for 0% -> 0% of each run, Pallas kernels for 0% -> 1%
where the time goes in v1:
time: 91 us; the launch traced here: 90.7 us
  blocking collectives  56 us (62%)
  Pallas kernels  20.9 us (23%)
  starting transfers between devices  5.47 us (6%)
  waiting for transfers between devices  4.46 us (5%)
  local copies, waits for them, and re-layouts  3.95 us (4%)
    all_to_all x1, blocking collectives, shards(): received = lax.all_to_all(merged, chips, 0, 0, tiled=False)  32.1 us
    all_to_all x1, blocking collectives, shards(): returned = lax.all_to_all(results, chips, 0, 0, tiled=False)  23.9 us
    pallas_call x1, Pallas kernels, shards(): pl.pallas_call(dispatch_kernel, grid=(clips,), in_specs=[pl.BlockSpec(mem...  9.36 us
    pallas_call x1, Pallas kernels, shards(): pl.pallas_call(mix_kernel, grid=(clips,), in_specs=[full, full, pl.BlockS...  4.96 us
    ppermute x1, starting transfers between devices, shards(): partner = lax.ppermute(returned, 'core', swap)  3.96 us
    unnamed x8, local copies, waits for them, and re-layouts  3.95 us
    pallas_call x1, Pallas kernels, shards(): pl.pallas_call(functools.partial(expert_kernel, 512), in_specs=[whole] *...  2.92 us
    ppermute x1, waiting for transfers between devices, shards(): theirs = lax.ppermute(other, 'core', swap)  2.85 us
  transfers between devices with their start and end apart: 2, of which 2 were waited for; matrix products, arithmetic and copies ran while one was open for 0% of the time, Pallas kernels for 1%

profile of v1, /device:TPU:1, one launch (start us, length us, event | category | flops | bytes accessed | tf_op | source)
XLA Modules:
  0.0 90.7 jit_solution(5620631186510769831)
XLA Ops:
  0.0 0.0 copy-start
  0.0 2.9 %copy-done = bf16[4,640,1280]{2,1,0:T(8,128)(2,1)S(1)} copy-done((bf16[4,640,1280]{2,1,0:T(8,128)(2,1)S(1)}, bf16[4,640,1280]{2,1,0:T(8,128)(2,1)}, u32[]{:S(2)}) %copy-start) | copy-done | bytes 6553624
  2.9 0.0 copy-start.3
  2.9 1.1 %copy-done.3 = bf16[1280,256]{1,0:T(8,128)(2,1)S(1)} copy-done((bf16[1280,256]{1,0:T(8,128)(2,1)S(1)}, bf16[1280,256]{1,0:T(8,128)(2,1)}, u32[]{:S(2)}) %copy-start.3) | copy-done | bytes 655384
  3.9 0.0 copy-start.2
  4.0 9.4 %shard_map.46 = (bf16[4,128,1408]{2,1,0:T(8,128)(2,1)S(1)}, bf16[4,128,1408]{2,1,0:T(8,128)(2,1)S(1)}, f32[4,640,256]{2,1,0:T(8,128)S(1)}) custom-call(s32[1]{0:T(128)} %bitcast.core_ref, bf16[4,640,1280]{2,1,0:T(8,128)(2,1)S(1)} %copy-done, bf16[1280,256]{1,0:T(8,128)(2,1)S(1)} %copy-done.3), custom_call_target="tpu_custom_call" | custom-call | tf_op jit(solution)/shard_map/pallas_call | solution.py:162
  13.3 1.5 %collective-permute-start = (bf16[4,128,1408]{2,1,0:T(8,128)(2,1)S(1)}, bf16[4,128,1408]{2,1,0:T(8,128)(2,1)S(1)}, u32[]{:S(2)}, u32[]{:S(2)}) collective-permute-start(bf16[4,128,1408]{2,1,0:T(8,128)(2,1)S(1)} %get-tuple-element.9), channel_id=1, source_target_pairs={{0,1},{1,0},{2,3},{3,2},{4,5},{5,4},{6,7},{7,6},{8,9},{9,8},{10,11... | collective-permute-start | bytes 4325384 | tf_op jit(solution)/shard_map/ppermute | solution.py:184
  14.8 2.8 %collective-permute-done.theirs_ref = bf16[4,128,1408]{2,1,0:T(8,128)(2,1)S(1)} collective-permute-done((bf16[4,128,1408]{2,1,0:T(8,128)(2,1)S(1)}, bf16[4,128,1408]{2,1,0:T(8,128)(2,1)S(1)}, u32[]{:S(2)}, u32[]{:S(2)}) %collective-permute-start) | collective-permute-done | bytes 1441824 | tf_op jit(solution)/shard_map/ppermute | solution.py:184
  17.7 0.0 copy-start.1
  17.7 2.6 %shard_map.47 = bf16[64,8,1408]{2,1,0:T(8,128)(2,1)S(1)} custom-call(bf16[4,128,1408]{2,1,0:T(8,128)(2,1)S(1)} %get-tuple-element.8.mine_ref, bf16[4,128,1408]{2,1,0:T(8,128)(2,1)S(1)} %collective-permute-done.theirs_ref), custom_call_target="tpu_custom_call" | custom-call | tf_op jit(solution)/shard_map/pallas_call | solution.py:186
  20.3 32.1 %all_to_all.10.received_ref = bf16[64,8,1408]{2,1,0:T(8,128)(2,1)S(1)} all-to-all(bf16[64,8,1408]{2,1,0:T(8,128)(2,1)S(1)} %shard_map.47), channel_id=1, replica_groups=mesh['x'=4,'z'=4,'y'=4,'core'=2] {'x','z','y'}, dimensions={0} | all-to-all | bytes 2883584 | tf_op jit(solution)/shard_map/all_to_all | solution.py:195
  52.3 0.0 copy-done.2
  52.3 0.0 copy-done.1
  52.3 2.9 %shard_map.48 = bf16[64,8,1280]{2,1,0:T(8,128)(2,1)S(1)} custom-call(bf16[64,8,1408]{2,1,0:T(8,128)(2,1)S(1)} %all_to_all.10.received_ref, bf16[1,1280,2560]{2,1,0:T(8,128)(2,1)S(1)} %copy-done.1, bf16[1,2560,1280]{2,1,0:T(8,128)(2,1)S(1)} %copy-done.2), custom_call_target="tpu_custom_call" | custom-call | tf_op jit(solution)/shard_map/pallas_call | solution.py:207
  55.3 23.9 %all_to_all.11.mine_ref = bf16[64,8,1280]{2,1,0:T(8,128)(2,1)S(1)} all-to-all(bf16[64,8,1280]{2,1,0:T(8,128)(2,1)S(1)} %shard_map.48), channel_id=1, replica_groups=mesh['x'=4,'z'=4,'y'=4,'core'=2] {'x','z','y'}, dimensions={0} | all-to-all | bytes 2621440 | tf_op jit(solution)/shard_map/all_to_all | solution.py:216
  79.2 4.0 %collective-permute-start.1 = (bf16[64,8,1280]{2,1,0:T(8,128)(2,1)S(1)}, bf16[64,8,1280]{2,1,0:T(8,128)(2,1)S(1)}, u32[]{:S(2)}, u32[]{:S(2)}) collective-permute-start(bf16[64,8,1280]{2,1,0:T(8,128)(2,1)S(1)} %all_to_all.11.mine_ref), channel_id=1, source_target_pairs={{0,1},{1,0},{2,3},{3,2},{4,5},{5,4},{6,7},{7,6},{8,9},{9,8},{10,11... | collective-permute-start | bytes 3932168 | tf_op jit(solution)/shard_map/ppermute | solution.py:217
  83.1 1.0 %shard_map.49.combine_ref = bf16[4,640,256]{2,1,0:T(8,128)(2,1)S(1)} custom-call(f32[4,640,256]{2,1,0:T(8,128)S(1)} %get-tuple-element.10.logits_ref), custom_call_target="tpu_custom_call" | custom-call | tf_op jit(solution)/shard_map/pallas_call | solution.py:197
  84.2 1.6 %collective-permute-done.1.theirs_ref = bf16[64,8,1280]{2,1,0:T(8,128)(2,1)S(1)} collective-permute-done((bf16[64,8,1280]{2,1,0:T(8,128)(2,1)S(1)}, bf16[64,8,1280]{2,1,0:T(8,128)(2,1)S(1)}, u32[]{:S(2)}, u32[]{:S(2)}) %collective-permute-start.1) | collective-permute-done | bytes 1310752 | tf_op jit(solution)/shard_map/ppermute | solution.py:217
  85.8 5.0 %shard_map.50 = bf16[4,640,1280]{2,1,0:T(8,128)(2,1)} custom-call(bf16[64,8,1280]{2,1,0:T(8,128)(2,1)S(1)} %all_to_all.11.mine_ref, bf16[64,8,1280]{2,1,0:T(8,128)(2,1)S(1)} %collective-permute-done.1.theirs_ref, bf16[4,640,256]{2,1,0:T(8,128)(2,1)S(1)} %shard_map.49.combine_ref), custom_call_target="tpu_custom_call" | custom-call | tf_op jit(solution)/shard_map/pallas_call | solution.py:220
Async XLA Ops:
  0.0 2.9 %copy-start = (bf16[4,640,1280]{2,1,0:T(8,128)(2,1)S(1)}, bf16[4,640,1280]{2,1,0:T(8,128)(2,1)}, u32[]{:S(2)}) copy-start(bf16[4,640,1280]{2,1,0:T(8,128)(2,1)} %tokens_ref.1) | copy-start | bytes 19660804
  2.9 1.1 %copy-start.3 = (bf16[1280,256]{1,0:T(8,128)(2,1)S(1)}, bf16[1280,256]{1,0:T(8,128)(2,1)}, u32[]{:S(2)}) copy-start(bf16[1280,256]{1,0:T(8,128)(2,1)} %router_ref.1) | copy-start | bytes 1966084
  3.9 48.4 %copy-start.2 = (bf16[1,2560,1280]{2,1,0:T(8,128)(2,1)S(1)}, bf16[1,2560,1280]{2,1,0:T(8,128)(2,1)}, u32[]{:S(2)}) copy-start(bf16[1,2560,1280]{2,1,0:T(8,128)(2,1)} %down_ref.1) | copy-start | bytes 19660804
  13.3 4.4 %collective-permute-start = (bf16[4,128,1408]{2,1,0:T(8,128)(2,1)S(1)}, bf16[4,128,1408]{2,1,0:T(8,128)(2,1)S(1)}, u32[]{:S(2)}, u32[]{:S(2)}) collective-permute-start(bf16[4,128,1408]{2,1,0:T(8,128)(2,1)S(1)} %get-tuple-element.9), channel_id=1, source_target_pairs={{0,1},{1,0},{2,3},{3,2},{4,5},{5,4},{6,7},{7,6},{8,9},{9,8},{10,11... | collective-permute-start | bytes 4325384 | tf_op jit(solution)/shard_map/ppermute | solution.py:184
  17.7 34.7 %copy-start.1 = (bf16[1,1280,2560]{2,1,0:T(8,128)(2,1)S(1)}, bf16[1,1280,2560]{2,1,0:T(8,128)(2,1)}, u32[]{:S(2)}) copy-start(bf16[1,1280,2560]{2,1,0:T(8,128)(2,1)} %up_ref.1) | copy-start | bytes 19660804
  79.2 6.6 %collective-permute-start.1 = (bf16[64,8,1280]{2,1,0:T(8,128)(2,1)S(1)}, bf16[64,8,1280]{2,1,0:T(8,128)(2,1)S(1)}, u32[]{:S(2)}, u32[]{:S(2)}) collective-permute-start(bf16[64,8,1280]{2,1,0:T(8,128)(2,1)S(1)} %all_to_all.11.mine_ref), channel_id=1, source_target_pairs={{0,1},{1,0},{2,3},{3,2},{4,5},{5,4},{6,7},{7,6},{8,9},{9,8},{10,11... | collective-permute-start | bytes 3932168 | tf_op jit(solution)/shard_map/ppermute | solution.py:217

commit v2 on v1

v2 whole, which is shorter than its diff:
```python
import functools

import jax
import jax.numpy as jnp
import numpy as np
from jax import lax
from jax.experimental import pallas as pl
from jax.experimental.pallas import tpu as pltpu
from jax.sharding import Mesh
from jax.sharding import PartitionSpec as P

F32, BF16 = jnp.float32, jnp.bfloat16
STAT = 128
CHIPS, PLACES, LINE, CORES = 64, 16, 4, 2
MIB = 1024 * 1024


def iota(shape, dim):
    return lax.broadcasted_iota(jnp.int32, shape, dim)


def pieces(value, count):
    out = []
    for _ in range(count):
        part = value.astype(BF16).astype(F32)
        out.append(part)
        value = value - part
    return out


def read_stats(stats):
    return stats[:, 0:1] + stats[:, 1:2] + stats[:, 2:3], stats[:, 3:4] + stats[:, 4:5]


def interleave(rows, back):
    new = iota((rows, rows), 1 if back else 0)
    old = iota((rows, rows), 0 if back else 1)
    place = (new // 2) % 4 * (rows // 4) + new // 8 * 2 + new % 2
    return jnp.where(old == place, 1.0, 0.0).astype(BF16)


def dispatch_kernel(
    core_ref, tokens_hbm, router_ref, mine_ref, other_ref, combine_ref, tokens_ref, ordered_ref, sems
):
    clips, _, depth = tokens_ref.shape
    slots = router_ref.shape[1]
    half = slots // CORES
    fetches = [pltpu.make_async_copy(tokens_hbm.at[c], tokens_ref.at[c], sems.at[c]) for c in range(clips)]
    for copy in fetches:
        copy.start()
    row, column = iota((slots, slots), 0), iota((slots, slots), 1)
    core = core_ref[0]
    owner = jnp.where(column < half, core, 1 - core)
    within = column % half
    source = within // 2 * 4 + owner * 2 + within % 2
    chosen = jnp.where(row == source, 1.0, 0.0).astype(BF16)
    ordered_ref[...] = jnp.dot(router_ref[...], chosen, preferred_element_type=F32).astype(BF16)

    def scores(c):
        fetches[c].wait()
        return jnp.dot(tokens_ref[c], ordered_ref[...], preferred_element_type=F32)

    def over_tokens(logits):
        top = jnp.max(logits, axis=0, keepdims=True)
        exponent = jnp.exp(logits - top)
        total = jnp.sum(exponent, axis=0, keepdims=True)
        rows = pieces(top, 3) + pieces(total, 2) + [1.0 / total]
        rows.append(jnp.zeros((STAT - len(rows), slots), F32))
        return exponent.astype(BF16), jnp.concatenate(rows, axis=0).T

    def over_slots(c, logits):
        exponent = jnp.exp(logits - jnp.max(logits, axis=1, keepdims=True))
        combine_ref[c] = (exponent * (1.0 / jnp.sum(exponent, axis=1, keepdims=True))).astype(BF16)

    def sums(c, exponent, stats):
        value = lax.dot_general(exponent, tokens_ref[c], (((0,), (0,)), ((), ())), preferred_element_type=F32)
        value = (value * stats[:, 5:6]).astype(BF16)
        stats = stats.astype(BF16)
        mine_ref[c, :, :depth] = value[:half]
        mine_ref[c, :, depth:] = stats[:half]
        other_ref[c, :, :depth] = value[half:]
        other_ref[c, :, depth:] = stats[half:]

    ahead, ready = scores(0), None
    for c in range(clips):
        logits = ahead
        if c + 1 < clips:
            ahead = scores(c + 1)
        fresh = over_tokens(logits)
        over_slots(c, logits)
        if ready is not None:
            sums(c - 1, *ready)
        ready = fresh
    sums(clips - 1, *ready)


def merge_kernel(mine_ref, theirs_ref, out_ref):
    clips, half, width = mine_ref.shape
    depth = width - STAT
    rows, part = 256, 256 // clips
    order = interleave(rows, False)
    for group in range(half // part):
        at = slice(group * part, group * part + part)
        to = slice(group * rows // 8, (group + 1) * rows // 8)

        def load(ref, lo, hi):
            return ref[:, at, lo:hi].astype(F32).reshape(rows, hi - lo)

        def store(lo, hi, value):
            moved = jnp.dot(order, value.astype(BF16), preferred_element_type=F32)
            out_ref[to, :, lo:hi] = moved.reshape(rows // 8, 8, hi - lo).astype(BF16)

        top_a, total_a = read_stats(load(mine_ref, depth, width))
        top_b, total_b = read_stats(load(theirs_ref, depth, width))
        top = jnp.maximum(top_a, top_b)
        weight_a = total_a * jnp.exp(top_a - top)
        weight_b = total_b * jnp.exp(top_b - top)
        total = weight_a + weight_b
        inverse = 1.0 / total
        lane = iota((rows, STAT), 1)
        stats = jnp.zeros((rows, STAT), F32)
        for k, value in enumerate(pieces(top, 3) + pieces(total, 2)):
            stats = jnp.where(lane == k, value, stats)
        store(depth, width, stats)
        weight_a, weight_b = weight_a * inverse, weight_b * inverse
        for lo in range(0, depth, 256):
            hi = lo + 256
            store(lo, hi, load(mine_ref, lo, hi) * weight_a + load(theirs_ref, lo, hi) * weight_b)


def expert_kernel(tile, received_ref, up_ref, down_ref, out_ref, rows_ref):
    depth = up_ref.shape[1]
    for place in range(PLACES):
        parts = [received_ref[place * LINE + y].astype(F32) for y in range(LINE)]
        stats = [read_stats(part[:, depth:]) for part in parts]
        top = functools.reduce(jnp.maximum, [s[0] for s in stats])
        weights = [s[1] * jnp.exp(s[0] - top) for s in stats]
        inverse = 1.0 / sum(weights)
        rows_ref[place * 8:place * 8 + 8, :] = sum(
            part[:, :depth] * (weight * inverse) for part, weight in zip(parts, weights)
        )
    rows = rows_ref[...].astype(BF16)
    result = jnp.zeros(rows.shape, F32)
    for start in range(0, up_ref.shape[2], tile):
        hidden = jnp.dot(rows, up_ref[0, :, start:start + tile], preferred_element_type=F32)
        hidden = (0.5 * hidden * (1.0 + lax.erf(hidden * np.float32(np.sqrt(0.5))))).astype(BF16)
        result = result + jnp.dot(hidden, down_ref[0, start:start + tile, :], preferred_element_type=F32)
    result = result.reshape(PLACES, 8, depth).astype(BF16)
    for place in range(PLACES):
        for y in range(LINE):
            out_ref[place * LINE + y] = result[place]


def by_clip(ref, out_ref):
    chips, lines, depth = ref.shape
    rows = 256
    order = interleave(rows, True)
    clips, part = 4, rows // 4
    for group in range(chips * lines // rows):
        for lo in range(0, depth, 256):
            block = ref[group * rows // 8:(group + 1) * rows // 8, :, lo:lo + 256]
            block = block.astype(F32).reshape(rows, 256).astype(BF16)
            moved = jnp.dot(order, block, preferred_element_type=F32).astype(BF16)
            out_ref[:, group * part:group * part + part, lo:lo + 256] = moved.reshape(clips, part, 256)


def mix_kernel(tile, mine_ref, theirs_ref, combine_ref, out_hbm, slots_ref, out_ref, sems):
    by_clip(theirs_ref, slots_ref)
    copies = []
    for c in range(combine_ref.shape[0]):
        slots = jnp.concatenate([mine_ref[c], slots_ref[c]], axis=0)
        for lo in range(0, combine_ref.shape[1], tile):
            out_ref[c, lo:lo + tile] = jnp.dot(
                combine_ref[c, lo:lo + tile], slots, preferred_element_type=F32
            ).astype(BF16)
            at = pl.ds(lo, tile)
            copy = pltpu.make_async_copy(out_ref.at[c, at], out_hbm.at[c, at], sems.at[len(copies)])
            copy.start()
            copies.append(copy)
    for copy in copies:
        copy.wait()


def params(mib):
    return pltpu.CompilerParams(vmem_limit_bytes=mib * MIB)


def shards(tokens, router, expert_up, expert_down):
    clips, count, depth = tokens.shape
    slots = router.shape[1]
    half = slots // CORES
    wide = depth + STAT
    core = lax.axis_index("core").astype(jnp.int32).reshape(1)
    swap = [(0, 1), (1, 0)]
    chips = ("x", "z", "y")

    whole = pl.BlockSpec(memory_space=pltpu.VMEM)
    far = pl.BlockSpec(memory_space=pltpu.HBM)

    mine, other, combine = pl.pallas_call(
        dispatch_kernel,
        in_specs=[pl.BlockSpec(memory_space=pltpu.SMEM), far, whole],
        out_specs=[whole] * 3,
        out_shape=[
            jax.ShapeDtypeStruct((clips, half, wide), BF16),
            jax.ShapeDtypeStruct((clips, half, wide), BF16),
            jax.ShapeDtypeStruct((clips, count, slots), BF16),
        ],
        scratch_shapes=[
            pltpu.VMEM((clips, count, depth), BF16),
            pltpu.VMEM((depth, slots), BF16),
            pltpu.SemaphoreType.DMA((clips,)),
        ],
        compiler_params=params(48),
    )(core, tokens, router)

    theirs = lax.ppermute(other, "core", swap)

    merged = pl.pallas_call(
        merge_kernel,
        in_specs=[whole] * 2,
        out_specs=whole,
        out_shape=jax.ShapeDtypeStruct((CHIPS, 8, wide), BF16),
        compiler_params=params(16),
    )(mine, theirs)

    received = lax.all_to_all(merged, chips, 0, 0, tiled=False)

    results = pl.pallas_call(
        functools.partial(expert_kernel, 512),
        in_specs=[whole] * 3,
        out_specs=whole,
        out_shape=jax.ShapeDtypeStruct((CHIPS, 8, depth), BF16),
        scratch_shapes=[pltpu.VMEM((PLACES * 8, depth), F32)],
        compiler_params=params(32),
    )(received, expert_up, expert_down)

    returned = lax.all_to_all(results, chips, 0, 0, tiled=False)
    partner = lax.ppermute(returned, "core", swap)

    own = pl.pallas_call(
        by_clip,
        in_specs=[whole],
        out_specs=whole,
        out_shape=jax.ShapeDtypeStruct((clips, half, depth), BF16),
        compiler_params=params(16),
    )(returned)

    tile = count // 2
    return pl.pallas_call(
        functools.partial(mix_kernel, tile),
        in_specs=[whole] * 3,
        out_specs=far,
        out_shape=jax.ShapeDtypeStruct((clips, count, depth), BF16),
        scratch_shapes=[
            pltpu.VMEM((clips, half, depth), BF16),
            pltpu.VMEM((clips, count, depth), BF16),
            pltpu.SemaphoreType.DMA((clips * 2,)),
        ],
        compiler_params=params(24),
    )(own, partner, combine)


def solution(mesh):
    fine = Mesh(np.asarray(mesh.devices).reshape(4, 4, LINE, CORES), ("x", "z", "y", "core"))
    in_specs = (
        P(("x", "z"), ("y", "core"), None),
        P(),
        P(("x", "z", "y", "core"), None, None),
        P(("x", "z", "y", "core"), None, None),
    )
    out_specs = P(("x", "z"), ("y", "core"), None)
    return jax.shard_map(shards, mesh=fine, in_specs=in_specs, out_specs=out_specs, check_vma=False)
```

time: 91 us -> 84.1 us (0.924)
  Pallas kernels: 20.9 us -> 16.1 us
  local copies, waits for them, and re-layouts: 3.95 us -> 1.09 us
    pallas_call x4, Pallas kernels: 17.9 us -> 13.1 us  [the longest x1 7.57 us: shards(): pl.pallas_call(dispatch_kernel, in_specs=[pl.BlockSpec(memory_space=pltpu...]
    unnamed x8 -> x6, local copies, waits for them, and re-layouts: 3.95 us -> 1.09 us
where the time goes in v2:
time: 84.1 us; the launch traced here: 83.9 us
  blocking collectives  56.1 us (67%)
  Pallas kernels  16.1 us (19%)
  starting transfers between devices  5.46 us (6%)
  waiting for transfers between devices  5 us (6%)
  local copies, waits for them, and re-layouts  1.09 us (1%)
    all_to_all x1, blocking collectives, shards(): received = lax.all_to_all(merged, chips, 0, 0, tiled=False)  32.2 us
    all_to_all x1, blocking collectives, shards(): returned = lax.all_to_all(results, chips, 0, 0, tiled=False)  23.9 us
    pallas_call x1, Pallas kernels, shards(): pl.pallas_call(dispatch_kernel, in_specs=[pl.BlockSpec(memory_space=pltpu...  7.57 us
    ppermute x1, starting transfers between devices, shards(): partner = lax.ppermute(returned, 'core', swap)  3.96 us
    pallas_call x1, Pallas kernels, shards(): pl.pallas_call(functools.partial(mix_kernel, tile), in_specs=[whole] * 3,...  3.59 us
    pallas_call x1, Pallas kernels, shards(): pl.pallas_call(functools.partial(expert_kernel, 512), in_specs=[whole] *...  2.94 us
    ppermute x1, waiting for transfers between devices, shards(): theirs = lax.ppermute(other, 'core', swap)  2.85 us
    ppermute x1, waiting for transfers between devices, shards(): partner = lax.ppermute(returned, 'core', swap)  2.15 us
  transfers between devices with their start and end apart: 2, of which 2 were waited for; matrix products, arithmetic and copies ran while one was open for 0% of the time, Pallas kernels for 1%

profile of v2, /device:TPU:1, one launch (start us, length us, event | category | flops | bytes accessed | tf_op | source)
XLA Modules:
  0.0 83.9 jit_solution(17161025736088085278)
XLA Ops:
  0.0 0.0 copy-start.2
  0.0 1.1 %copy-done.2 = bf16[1280,256]{1,0:T(8,128)(2,1)S(1)} copy-done((bf16[1280,256]{1,0:T(8,128)(2,1)S(1)}, bf16[1280,256]{1,0:T(8,128)(2,1)}, u32[]{:S(2)}) %copy-start.2) | copy-done | bytes 655384
  1.1 0.0 copy-start.1
  1.1 7.6 %shard_map.46 = (bf16[4,128,1408]{2,1,0:T(8,128)(2,1)S(1)}, bf16[4,128,1408]{2,1,0:T(8,128)(2,1)S(1)}, bf16[4,640,256]{2,1,0:T(8,128)(2,1)S(1)}) custom-call(s32[1]{0:T(128)} %bitcast.core_ref, bf16[4,640,1280]{2,1,0:T(8,128)(2,1)} %tokens_hbm.1, bf16[1280,256]{1,0:T(8,128)(2,1)S(1)} %copy-done.2), custom_call_target="tpu_custom_call" | custom-call | tf_op jit(solution)/shard_map/pallas_call | solution.py:200
  8.7 1.5 %collective-permute-start = (bf16[4,128,1408]{2,1,0:T(8,128)(2,1)S(1)}, bf16[4,128,1408]{2,1,0:T(8,128)(2,1)S(1)}, u32[]{:S(2)}, u32[]{:S(2)}) collective-permute-start(bf16[4,128,1408]{2,1,0:T(8,128)(2,1)S(1)} %get-tuple-element.9), channel_id=1, source_target_pairs={{0,1},{1,0},{2,3},{3,2},{4,5},{5,4},{6,7},{7,6},{8,9},{9,8},{10,11... | collective-permute-start | bytes 4325384 | tf_op jit(solution)/shard_map/ppermute | solution.py:217
  10.2 2.8 %collective-permute-done.theirs_ref = bf16[4,128,1408]{2,1,0:T(8,128)(2,1)S(1)} collective-permute-done((bf16[4,128,1408]{2,1,0:T(8,128)(2,1)S(1)}, bf16[4,128,1408]{2,1,0:T(8,128)(2,1)S(1)}, u32[]{:S(2)}, u32[]{:S(2)}) %collective-permute-start) | collective-permute-done | bytes 1441824 | tf_op jit(solution)/shard_map/ppermute | solution.py:217
  13.0 0.0 copy-start
  13.0 1.5 %shard_map.47 = bf16[64,8,1408]{2,1,0:T(8,128)(2,1)S(1)} custom-call(bf16[4,128,1408]{2,1,0:T(8,128)(2,1)S(1)} %get-tuple-element.8.mine_ref, bf16[4,128,1408]{2,1,0:T(8,128)(2,1)S(1)} %collective-permute-done.theirs_ref), custom_call_target="tpu_custom_call" | custom-call | tf_op jit(solution)/shard_map/pallas_call | solution.py:219
  14.5 32.2 %all_to_all.10.received_ref = bf16[64,8,1408]{2,1,0:T(8,128)(2,1)S(1)} all-to-all(bf16[64,8,1408]{2,1,0:T(8,128)(2,1)S(1)} %shard_map.47), channel_id=1, replica_groups=mesh['x'=4,'z'=4,'y'=4,'core'=2] {'x','z','y'}, dimensions={0} | all-to-all | bytes 2883584 | tf_op jit(solution)/shard_map/all_to_all | solution.py:227
  46.7 0.0 copy-done.1
  46.7 0.0 copy-done
  46.7 2.9 %shard_map.48 = bf16[64,8,1280]{2,1,0:T(8,128)(2,1)S(1)} custom-call(bf16[64,8,1408]{2,1,0:T(8,128)(2,1)S(1)} %all_to_all.10.received_ref, bf16[1,1280,2560]{2,1,0:T(8,128)(2,1)S(1)} %copy-done, bf16[1,2560,1280]{2,1,0:T(8,128)(2,1)S(1)} %copy-done.1), custom_call_target="tpu_custom_call" | custom-call | tf_op jit(solution)/shard_map/pallas_call | solution.py:229
  49.6 23.9 %all_to_all.11.ref = bf16[64,8,1280]{2,1,0:T(8,128)(2,1)S(1)} all-to-all(bf16[64,8,1280]{2,1,0:T(8,128)(2,1)S(1)} %shard_map.48), channel_id=1, replica_groups=mesh['x'=4,'z'=4,'y'=4,'core'=2] {'x','z','y'}, dimensions={0} | all-to-all | bytes 2621440 | tf_op jit(solution)/shard_map/all_to_all | solution.py:238
  73.5 4.0 %collective-permute-start.1 = (bf16[64,8,1280]{2,1,0:T(8,128)(2,1)S(1)}, bf16[64,8,1280]{2,1,0:T(8,128)(2,1)S(1)}, u32[]{:S(2)}, u32[]{:S(2)}) collective-permute-start(bf16[64,8,1280]{2,1,0:T(8,128)(2,1)S(1)} %all_to_all.11.ref), channel_id=1, source_target_pairs={{0,1},{1,0},{2,3},{3,2},{4,5},{5,4},{6,7},{7,6},{8,9},{9,8},{10,11... | collective-permute-start | bytes 3932168 | tf_op jit(solution)/shard_map/ppermute | solution.py:239
  77.5 0.5 shard_map.49.mine_ref
  78.0 2.1 %collective-permute-done.1.theirs_ref = bf16[64,8,1280]{2,1,0:T(8,128)(2,1)S(1)} collective-permute-done((bf16[64,8,1280]{2,1,0:T(8,128)(2,1)S(1)}, bf16[64,8,1280]{2,1,0:T(8,128)(2,1)S(1)}, u32[]{:S(2)}, u32[]{:S(2)}) %collective-permute-start.1) | collective-permute-done | bytes 1310752 | tf_op jit(solution)/shard_map/ppermute | solution.py:239
  80.2 3.6 %shard_map.50 = bf16[4,640,1280]{2,1,0:T(8,128)(2,1)} custom-call(bf16[4,128,1280]{2,1,0:T(8,128)(2,1)S(1)} %shard_map.49.mine_ref, bf16[64,8,1280]{2,1,0:T(8,128)(2,1)S(1)} %collective-permute-done.1.theirs_ref, bf16[4,640,256]{2,1,0:T(8,128)(2,1)S(1)} %get-tuple-element.10.combine_ref), custom_call_target="tpu_custom_call" | custom-call | tf_op jit(solution)/shard_map/pallas_call | solution.py:250
Async XLA Ops:
  0.0 1.1 %copy-start.2 = (bf16[1280,256]{1,0:T(8,128)(2,1)S(1)}, bf16[1280,256]{1,0:T(8,128)(2,1)}, u32[]{:S(2)}) copy-start(bf16[1280,256]{1,0:T(8,128)(2,1)} %router_ref.1) | copy-start | bytes 1966084
  1.1 45.6 %copy-start.1 = (bf16[1,2560,1280]{2,1,0:T(8,128)(2,1)S(1)}, bf16[1,2560,1280]{2,1,0:T(8,128)(2,1)}, u32[]{:S(2)}) copy-start(bf16[1,2560,1280]{2,1,0:T(8,128)(2,1)} %down_ref.1) | copy-start | bytes 19660804
  8.7 4.4 %collective-permute-start = (bf16[4,128,1408]{2,1,0:T(8,128)(2,1)S(1)}, bf16[4,128,1408]{2,1,0:T(8,128)(2,1)S(1)}, u32[]{:S(2)}, u32[]{:S(2)}) collective-permute-start(bf16[4,128,1408]{2,1,0:T(8,128)(2,1)S(1)} %get-tuple-element.9), channel_id=1, source_target_pairs={{0,1},{1,0},{2,3},{3,2},{4,5},{5,4},{6,7},{7,6},{8,9},{9,8},{10,11... | collective-permute-start | bytes 4325384 | tf_op jit(solution)/shard_map/ppermute | solution.py:217
  13.0 33.6 %copy-start = (bf16[1,1280,2560]{2,1,0:T(8,128)(2,1)S(1)}, bf16[1,1280,2560]{2,1,0:T(8,128)(2,1)}, u32[]{:S(2)}) copy-start(bf16[1,1280,2560]{2,1,0:T(8,128)(2,1)} %up_ref.1) | copy-start | bytes 19660804
  73.5 6.6 %collective-permute-start.1 = (bf16[64,8,1280]{2,1,0:T(8,128)(2,1)S(1)}, bf16[64,8,1280]{2,1,0:T(8,128)(2,1)S(1)}, u32[]{:S(2)}, u32[]{:S(2)}) collective-permute-start(bf16[64,8,1280]{2,1,0:T(8,128)(2,1)S(1)} %all_to_all.11.ref), channel_id=1, source_target_pairs={{0,1},{1,0},{2,3},{3,2},{4,5},{5,4},{6,7},{7,6},{8,9},{9,8},{10,11... | collective-permute-start | bytes 3932168 | tf_op jit(solution)/shard_map/ppermute | solution.py:239

commit v3 on v2

--- a/solution.py
+++ b/solution.py
@@ -39,10 +39,26 @@
     return jnp.where(old == place, 1.0, 0.0).astype(BF16)
 
 
-def dispatch_kernel(
-    core_ref, tokens_hbm, router_ref, mine_ref, other_ref, combine_ref, tokens_ref, ordered_ref, sems
+def stats_columns(logits):
+    top = jnp.max(logits, axis=0, keepdims=True)
+    exponent = jnp.exp(logits - top)
+    total = jnp.sum(exponent, axis=0, keepdims=True)
+    rows = pieces(top, 3) + pieces(total, 2) + [1.0 / total]
+    rows.append(jnp.zeros((STAT - len(rows), logits.shape[1]), F32))
+    return exponent.astype(BF16), jnp.concatenate(rows, axis=0).T
+
+
+def store_sums(out_ref, c, exponent, stats, tokens):
+    depth = tokens.shape[1]
+    value = lax.dot_general(exponent, tokens, (((0,), (0,)), ((), ())), preferred_element_type=F32)
+    out_ref[c, :, :depth] = (value * stats[:, 5:6]).astype(BF16)
+    out_ref[c, :, depth:] = stats.astype(BF16)
+
+
+def scores_kernel(
+    core_ref, tokens_hbm, router_ref, other_ref, tokens_ref, logits_ref, ordered_ref, sems
 ):
-    clips, _, depth = tokens_ref.shape
+    clips = tokens_ref.shape[0]
     slots = router_ref.shape[1]
     half = slots // CORES
     fetches = [pltpu.make_async_copy(tokens_hbm.at[c], tokens_ref.at[c], sems.at[c]) for c in range(clips)]
@@ -57,41 +73,32 @@
     ordered_ref[...] = jnp.dot(router_ref[...], chosen, preferred_element_type=F32).astype(BF16)
 
     def scores(c):
-        fetches[c].wait()
-        return jnp.dot(tokens_ref[c], ordered_ref[...], preferred_element_type=F32)
-
-    def over_tokens(logits):
-        top = jnp.max(logits, axis=0, keepdims=True)
-        exponent = jnp.exp(logits - top)
-        total = jnp.sum(exponent, axis=0, keepdims=True)
-        rows = pieces(top, 3) + pieces(total, 2) + [1.0 / total]
-        rows.append(jnp.zeros((STAT - len(rows), slots), F32))
-        return exponent.astype(BF16), jnp.concatenate(rows, axis=0).T
-
-    def over_slots(c, logits):
+        logits_ref[c] = jnp.dot(tokens_ref[c], ordered_ref[...], preferred_element_type=F32)
+
+    def rest(c):
+        store_sums(other_ref, c, *stats_columns(logits_ref[c, :, half:]), tokens_ref[c])
+
+    for copy in fetches[:2]:
+        copy.wait()
+    scores(0)
+    scores(1)
+    rest(0)
+    for copy in fetches[2:]:
+        copy.wait()
+    scores(2)
+    rest(1)
+    scores(3)
+    rest(2)
+    rest(3)
+
+
+def sums_kernel(tokens_ref, logits_ref, mine_ref, combine_ref):
+    half = mine_ref.shape[1]
+    for c in range(tokens_ref.shape[0]):
+        logits = logits_ref[c]
+        store_sums(mine_ref, c, *stats_columns(logits[:, :half]), tokens_ref[c])
         exponent = jnp.exp(logits - jnp.max(logits, axis=1, keepdims=True))
         combine_ref[c] = (exponent * (1.0 / jnp.sum(exponent, axis=1, keepdims=True))).astype(BF16)
-
-    def sums(c, exponent, stats):
-        value = lax.dot_general(exponent, tokens_ref[c], (((0,), (0,)), ((), ())), preferred_element_type=F32)
-        value = (value * stats[:, 5:6]).astype(BF16)
-        stats = stats.astype(BF16)
-        mine_ref[c, :, :depth] = value[:half]
-        mine_ref[c, :, depth:] = stats[:half]
-        other_ref[c, :, :depth] = value[half:]
-        other_ref[c, :, depth:] = stats[half:]
-
-    ahead, ready = scores(0), None
-    for c in range(clips):
-        logits = ahead
-        if c + 1 < clips:
-            ahead = scores(c + 1)
-        fresh = over_tokens(logits)
-        over_slots(c, logits)
-        if ready is not None:
-            sums(c - 1, *ready)
-        ready = fresh
-    sums(clips - 1, *ready)
 
 
 def merge_kernel(mine_ref, theirs_ref, out_ref):
@@ -128,8 +135,8 @@
             store(lo, hi, load(mine_ref, lo, hi) * weight_a + load(theirs_ref, lo, hi) * weight_b)
 
 
-def expert_kernel(tile, received_ref, up_ref, down_ref, out_ref, rows_ref):
-    depth = up_ref.shape[1]
+def expert_kernel(tile, received_ref, up_ref, down_ref, out_ref, rows_ref, hidden_ref):
+    depth, hidden = up_ref.shape[1:]
     for place in range(PLACES):
         parts = [received_ref[place * LINE + y].astype(F32) for y in range(LINE)]
         stats = [read_stats(part[:, depth:]) for part in parts]
@@ -140,15 +147,17 @@
             part[:, :depth] * (weight * inverse) for part, weight in zip(parts, weights)
         )
     rows = rows_ref[...].astype(BF16)
-    result = jnp.zeros(rows.shape, F32)
-    for start in range(0, up_ref.shape[2], tile):
-        hidden = jnp.dot(rows, up_ref[0, :, start:start + tile], preferred_element_type=F32)
-        hidden = (0.5 * hidden * (1.0 + lax.erf(hidden * np.float32(np.sqrt(0.5))))).astype(BF16)
-        result = result + jnp.dot(hidden, down_ref[0, start:start + tile, :], preferred_element_type=F32)
-    result = result.reshape(PLACES, 8, depth).astype(BF16)
-    for place in range(PLACES):
-        for y in range(LINE):
-            out_ref[place * LINE + y] = result[place]
+    for lo in range(0, hidden, 2 * tile):
+        hi = lo + 2 * tile
+        value = jnp.dot(rows, up_ref[0, :, lo:hi], preferred_element_type=F32)
+        hidden_ref[:, lo:hi] = (0.5 * value * (1.0 + lax.erf(value * np.float32(np.sqrt(0.5))))).astype(BF16)
+    for lo in range(0, depth, tile):
+        hi = lo + tile
+        result = jnp.dot(hidden_ref[...], down_ref[0, :, lo:hi], preferred_element_type=F32)
+        result = result.reshape(PLACES, 8, tile).astype(BF16)
+        for place in range(PLACES):
+            for y in range(LINE):
+                out_ref[place * LINE + y, :, lo:hi] = result[place]
 
 
 def by_clip(ref, out_ref):
@@ -197,24 +206,31 @@
     whole = pl.BlockSpec(memory_space=pltpu.VMEM)
     far = pl.BlockSpec(memory_space=pltpu.HBM)
 
-    mine, other, combine = pl.pallas_call(
-        dispatch_kernel,
+    other, near, logits = pl.pallas_call(
+        scores_kernel,
         in_specs=[pl.BlockSpec(memory_space=pltpu.SMEM), far, whole],
         out_specs=[whole] * 3,
         out_shape=[
             jax.ShapeDtypeStruct((clips, half, wide), BF16),
+            jax.ShapeDtypeStruct((clips, count, depth), BF16),
+            jax.ShapeDtypeStruct((clips, count, slots), F32),
+        ],
+        scratch_shapes=[pltpu.VMEM((depth, slots), BF16), pltpu.SemaphoreType.DMA((clips,))],
+        compiler_params=params(39),
+    )(core, tokens, router)
+
+    theirs = lax.ppermute(other, "core", swap)
+
+    mine, combine = pl.pallas_call(
+        sums_kernel,
+        in_specs=[whole] * 2,
+        out_specs=[whole] * 2,
+        out_shape=[
             jax.ShapeDtypeStruct((clips, half, wide), BF16),
             jax.ShapeDtypeStruct((clips, count, slots), BF16),
         ],
-        scratch_shapes=[
-            pltpu.VMEM((clips, count, depth), BF16),
-            pltpu.VMEM((depth, slots), BF16),
-            pltpu.SemaphoreType.DMA((clips,)),
-        ],
-        compiler_params=params(48),
-    )(core, tokens, router)
-
-    theirs = lax.ppermute(other, "core", swap)
+        compiler_params=params(16),
+    )(near, logits)
 
     merged = pl.pallas_call(
         merge_kernel,
@@ -227,11 +243,11 @@
     received = lax.all_to_all(merged, chips, 0, 0, tiled=False)
 
     results = pl.pallas_call(
-        functools.partial(expert_kernel, 512),
+        functools.partial(expert_kernel, 256),
         in_specs=[whole] * 3,
         out_specs=whole,
         out_shape=jax.ShapeDtypeStruct((CHIPS, 8, depth), BF16),
-        scratch_shapes=[pltpu.VMEM((PLACES * 8, depth), F32)],
+        scratch_shapes=[pltpu.VMEM((PLACES * 8, depth), F32), pltpu.VMEM((PLACES * 8, expert_up.shape[2]), BF16)],
         compiler_params=params(32),
     )(received, expert_up, expert_down)
 

time: 84.1 us -> 82 us (0.975)
  waiting for transfers between devices: 5 us -> 3.28 us
    ppermute x1, waiting for transfers between devices: 2.85 us -> 1.14 us  [shards(): theirs = lax.ppermute(other, 'core', swap)]
    pallas_call x2 -> x3, Pallas kernels: 10.5 us -> 10.2 us  [the longest x1 6.05 us: shards(): pl.pallas_call(scores_kernel, in_specs=[pl.BlockSpec(memory_space=pltpu.S...]
  transfers between devices with their start and end apart: 2 -> 2, of which waited for: 2 -> 2; matrix products, arithmetic and copies ran while one was open for 0% -> 0% of each run, Pallas kernels for 1% -> 3%
where the time goes in v3:
time: 82 us; the launch traced here: 81.8 us
  blocking collectives  56 us (68%)
  Pallas kernels  15.7 us (19%)
  starting transfers between devices  5.46 us (7%)
  waiting for transfers between devices  3.28 us (4%)
  local copies, waits for them, and re-layouts  1.1 us (1%)
    all_to_all x1, blocking collectives, shards(): received = lax.all_to_all(merged, chips, 0, 0, tiled=False)  32.1 us
    all_to_all x1, blocking collectives, shards(): returned = lax.all_to_all(results, chips, 0, 0, tiled=False)  23.9 us
    pallas_call x1, Pallas kernels, shards(): pl.pallas_call(scores_kernel, in_specs=[pl.BlockSpec(memory_space=pltpu.S...  6.05 us
    ppermute x1, starting transfers between devices, shards(): partner = lax.ppermute(returned, 'core', swap)  3.96 us
    pallas_call x1, Pallas kernels, shards(): pl.pallas_call(functools.partial(mix_kernel, tile), in_specs=[whole] * 3,...  3.59 us
    pallas_call x1, Pallas kernels, shards(): pl.pallas_call(functools.partial(expert_kernel, 256), in_specs=[whole] *...  2.44 us
    ppermute x1, waiting for transfers between devices, shards(): partner = lax.ppermute(returned, 'core', swap)  2.15 us
    pallas_call x1, Pallas kernels, shards(): pl.pallas_call(sums_kernel, in_specs=[whole] * 2, out_specs=[whole] * 2,...  1.7 us
  transfers between devices with their start and end apart: 2, of which 2 were waited for; matrix products, arithmetic and copies ran while one was open for 0% of the time, Pallas kernels for 3%

profile of v3, /device:TPU:1, one launch (start us, length us, event | category | flops | bytes accessed | tf_op | source)
XLA Modules:
  0.0 81.8 jit_solution(4441153236798171563)
XLA Ops:
  0.0 0.0 copy-start
  0.0 1.1 %copy-done = bf16[1280,256]{1,0:T(8,128)(2,1)S(1)} copy-done((bf16[1280,256]{1,0:T(8,128)(2,1)S(1)}, bf16[1280,256]{1,0:T(8,128)(2,1)}, u32[]{:S(2)}) %copy-start) | copy-done | bytes 655384
  1.1 0.0 slice-start
  1.1 0.0 slice-start.2
  1.1 6.0 %shard_map.46 = (bf16[4,128,1408]{2,1,0:T(8,128)(2,1)S(1)}, bf16[4,640,1280]{2,1,0:T(8,128)(2,1)S(1)}, f32[4,640,256]{2,1,0:T(8,128)S(1)}) custom-call(s32[1]{0:T(128)} %bitcast.core_ref, bf16[4,640,1280]{2,1,0:T(8,128)(2,1)} %tokens_hbm.1, bf16[1280,256]{1,0:T(8,128)(2,1)S(1)} %copy-done), custom_call_target="tpu_custom_call" | custom-call | tf_op jit(solution)/shard_map/pallas_call | solution.py:209
  7.1 1.5 %collective-permute-start = (bf16[4,128,1408]{2,1,0:T(8,128)(2,1)S(1)}, bf16[4,128,1408]{2,1,0:T(8,128)(2,1)S(1)}, u32[]{:S(2)}, u32[]{:S(2)}) collective-permute-start(bf16[4,128,1408]{2,1,0:T(8,128)(2,1)S(1)} %get-tuple-element.13), channel_id=1, source_target_pairs={{0,1},{1,0},{2,3},{3,2},{4,5},{5,4},{6,7},{7,6},{8,9},{9,8},{10,11... | collective-permute-start | bytes 4325384 | tf_op jit(solution)/shard_map/ppermute | solution.py:222
  8.6 0.0 slice-start.1
  8.7 0.0 slice-start.3
  8.7 1.7 %shard_map.47 = (bf16[4,128,1408]{2,1,0:T(8,128)(2,1)S(1)}, bf16[4,640,256]{2,1,0:T(8,128)(2,1)S(1)}) custom-call(bf16[4,640,1280]{2,1,0:T(8,128)(2,1)S(1)} %get-tuple-element.10.tokens_ref, f32[4,640,256]{2,1,0:T(8,128)S(1)} %get-tuple-element.11.logits_ref), custom_call_target="tpu_custom_call" | custom-call | tf_op jit(solution)/shard_map/pallas_call | solution.py:224
  10.4 1.1 %collective-permute-done.theirs_ref = bf16[4,128,1408]{2,1,0:T(8,128)(2,1)S(1)} collective-permute-done((bf16[4,128,1408]{2,1,0:T(8,128)(2,1)S(1)}, bf16[4,128,1408]{2,1,0:T(8,128)(2,1)S(1)}, u32[]{:S(2)}, u32[]{:S(2)}) %collective-permute-start) | collective-permute-done | bytes 1441824 | tf_op jit(solution)/shard_map/ppermute | solution.py:222
  11.5 1.4 %shard_map.48 = bf16[64,8,1408]{2,1,0:T(8,128)(2,1)S(1)} custom-call(bf16[4,128,1408]{2,1,0:T(8,128)(2,1)S(1)} %get-tuple-element.12.mine_ref, bf16[4,128,1408]{2,1,0:T(8,128)(2,1)S(1)} %collective-permute-done.theirs_ref), custom_call_target="tpu_custom_call" | custom-call | tf_op jit(solution)/shard_map/pallas_call | solution.py:235
  12.9 32.1 %all_to_all.10.received_ref = bf16[64,8,1408]{2,1,0:T(8,128)(2,1)S(1)} all-to-all(bf16[64,8,1408]{2,1,0:T(8,128)(2,1)S(1)} %shard_map.48), channel_id=1, replica_groups=mesh['x'=4,'z'=4,'y'=4,'core'=2] {'x','z','y'}, dimensions={0} | all-to-all | bytes 2883584 | tf_op jit(solution)/shard_map/all_to_all | solution.py:243
  45.0 0.0 slice-done
  45.0 0.0 slice-done.2
  45.0 0.0 slice-done.1
  45.0 0.0 slice-done.3
  45.0 2.4 %shard_map.49 = bf16[64,8,1280]{2,1,0:T(8,128)(2,1)S(1)} custom-call(bf16[64,8,1408]{2,1,0:T(8,128)(2,1)S(1)} %all_to_all.10.received_ref, bf16[1,1280,2560]{2,1,0:T(8,128)(2,1)S(1)} %bitcast.2, bf16[1,2560,1280]{2,1,0:T(8,128)(2,1)S(1)} %bitcast.4), custom_call_target="tpu_custom_call" | custom-call | tf_op jit(solution)/shard_map/pallas_call | solution.py:245
  47.5 23.9 %all_to_all.11.ref = bf16[64,8,1280]{2,1,0:T(8,128)(2,1)S(1)} all-to-all(bf16[64,8,1280]{2,1,0:T(8,128)(2,1)S(1)} %shard_map.49), channel_id=1, replica_groups=mesh['x'=4,'z'=4,'y'=4,'core'=2] {'x','z','y'}, dimensions={0} | all-to-all | bytes 2621440 | tf_op jit(solution)/shard_map/all_to_all | solution.py:254
  71.4 4.0 %collective-permute-start.1 = (bf16[64,8,1280]{2,1,0:T(8,128)(2,1)S(1)}, bf16[64,8,1280]{2,1,0:T(8,128)(2,1)S(1)}, u32[]{:S(2)}, u32[]{:S(2)}) collective-permute-start(bf16[64,8,1280]{2,1,0:T(8,128)(2,1)S(1)} %all_to_all.11.ref), channel_id=1, source_target_pairs={{0,1},{1,0},{2,3},{3,2},{4,5},{5,4},{6,7},{7,6},{8,9},{9,8},{10,11... | collective-permute-start | bytes 3932168 | tf_op jit(solution)/shard_map/ppermute | solution.py:255
  75.3 0.5 shard_map.50.mine_ref
  75.9 2.1 %collective-permute-done.1.theirs_ref = bf16[64,8,1280]{2,1,0:T(8,128)(2,1)S(1)} collective-permute-done((bf16[64,8,1280]{2,1,0:T(8,128)(2,1)S(1)}, bf16[64,8,1280]{2,1,0:T(8,128)(2,1)S(1)}, u32[]{:S(2)}, u32[]{:S(2)}) %collective-permute-start.1) | collective-permute-done | bytes 1310752 | tf_op jit(solution)/shard_map/ppermute | solution.py:255
  78.0 3.6 %shard_map.51 = bf16[4,640,1280]{2,1,0:T(8,128)(2,1)} custom-call(bf16[4,128,1280]{2,1,0:T(8,128)(2,1)S(1)} %shard_map.50.mine_ref, bf16[64,8,1280]{2,1,0:T(8,128)(2,1)S(1)} %collective-permute-done.1.theirs_ref, bf16[4,640,256]{2,1,0:T(8,128)(2,1)S(1)} %get-tuple-element.14.combine_ref), custom_call_target="tpu_custom_call" | custom-call | tf_op jit(solution)/shard_map/pallas_call | solution.py:266
  (2 shorter events, 0.0 us)
Async XLA Ops:
  0.0 1.1 %copy-start = (bf16[1280,256]{1,0:T(8,128)(2,1)S(1)}, bf16[1280,256]{1,0:T(8,128)(2,1)}, u32[]{:S(2)}) copy-start(bf16[1280,256]{1,0:T(8,128)(2,1)} %router_ref.1) | copy-start | bytes 1966084
  1.1 43.9 %slice-start = ((s8[6553600]{0:T(1024)(128)(4,1)}), s8[2359296]{0:T(1024)(128)(4,1)S(1)}, s32[]{:S(2)}) async-start(s8[6553600]{0:T(1024)(128)(4,1)} %bitcast.1), calls=%async_computation.2 | async-start | bytes 4718592
  1.1 43.9 %slice-start.2 = ((s8[6553600]{0:T(1024)(128)(4,1)}), s8[4194304]{0:T(1024)(128)(4,1)S(1)}, s32[]{:S(2)}) async-start(s8[6553600]{0:T(1024)(128)(4,1)} %bitcast.3), calls=%async_computation.4 | async-start | bytes 8388608
  7.1 4.4 %collective-permute-start = (bf16[4,128,1408]{2,1,0:T(8,128)(2,1)S(1)}, bf16[4,128,1408]{2,1,0:T(8,128)(2,1)S(1)}, u32[]{:S(2)}, u32[]{:S(2)}) collective-permute-start(bf16[4,128,1408]{2,1,0:T(8,128)(2,1)S(1)} %get-tuple-element.13), channel_id=1, source_target_pairs={{0,1},{1,0},{2,3},{3,2},{4,5},{5,4},{6,7},{7,6},{8,9},{9,8},{10,11... | collective-permute-start | bytes 4325384 | tf_op jit(solution)/shard_map/ppermute | solution.py:222
  8.6 36.3 %slice-start.1 = ((s8[6553600]{0:T(1024)(128)(4,1)}), s8[4194304]{0:T(1024)(128)(4,1)S(1)}, s32[]{:S(2)}) async-start(s8[6553600]{0:T(1024)(128)(4,1)} %bitcast.1), calls=%async_computation.3 | async-start | bytes 8388608
  8.7 36.3 %slice-start.3 = ((s8[6553600]{0:T(1024)(128)(4,1)}), s8[2359296]{0:T(1024)(128)(4,1)S(1)}, s32[]{:S(2)}) async-start(s8[6553600]{0:T(1024)(128)(4,1)} %bitcast.3), calls=%async_computation.5 | async-start | bytes 4718592
  71.4 6.6 %collective-permute-start.1 = (bf16[64,8,1280]{2,1,0:T(8,128)(2,1)S(1)}, bf16[64,8,1280]{2,1,0:T(8,128)(2,1)S(1)}, u32[]{:S(2)}, u32[]{:S(2)}) collective-permute-start(bf16[64,8,1280]{2,1,0:T(8,128)(2,1)S(1)} %all_to_all.11.ref), channel_id=1, source_target_pairs={{0,1},{1,0},{2,3},{3,2},{4,5},{5,4},{6,7},{7,6},{8,9},{9,8},{10,11... | collective-permute-start | bytes 3932168 | tf_op jit(solution)/shard_map/ppermute | solution.py:255

commit v4 on v3

--- a/solution.py
+++ b/solution.py
@@ -55,14 +55,26 @@
     out_ref[c, :, depth:] = stats.astype(BF16)
 
 
-def scores_kernel(
-    core_ref, tokens_hbm, router_ref, other_ref, tokens_ref, logits_ref, ordered_ref, sems
+def scores(tokens_ref, ordered_ref, other_ref, logits_ref, first):
+    clips, _, slots = logits_ref.shape
+    half = slots // CORES
+    for c in range(clips):
+        logits_ref[c] = jnp.dot(tokens_ref[first + c], ordered_ref[...], preferred_element_type=F32)
+    for c in range(clips):
+        store_sums(other_ref, c, *stats_columns(logits_ref[c, :, half:]), tokens_ref[first + c])
+
+
+def first_scores_kernel(
+    core_ref, tokens_hbm, router_hbm, other_ref, tokens_ref, logits_ref, ordered_ref, router_ref, sems
 ):
     clips = tokens_ref.shape[0]
+    now = logits_ref.shape[0]
     slots = router_ref.shape[1]
     half = slots // CORES
     fetches = [pltpu.make_async_copy(tokens_hbm.at[c], tokens_ref.at[c], sems.at[c]) for c in range(clips)]
-    for copy in fetches:
+    fetch = pltpu.make_async_copy(router_hbm, router_ref, sems.at[clips])
+    fetch.start()
+    for copy in fetches[:now]:
         copy.start()
     row, column = iota((slots, slots), 0), iota((slots, slots), 1)
     core = core_ref[0]
@@ -70,38 +82,32 @@
     within = column % half
     source = within // 2 * 4 + owner * 2 + within % 2
     chosen = jnp.where(row == source, 1.0, 0.0).astype(BF16)
+    fetch.wait()
+    for copy in fetches[now:]:
+        copy.start()
     ordered_ref[...] = jnp.dot(router_ref[...], chosen, preferred_element_type=F32).astype(BF16)
-
-    def scores(c):
-        logits_ref[c] = jnp.dot(tokens_ref[c], ordered_ref[...], preferred_element_type=F32)
-
-    def rest(c):
-        store_sums(other_ref, c, *stats_columns(logits_ref[c, :, half:]), tokens_ref[c])
-
-    for copy in fetches[:2]:
+    for copy in fetches[:now]:
         copy.wait()
-    scores(0)
-    scores(1)
-    rest(0)
-    for copy in fetches[2:]:
+    scores(tokens_ref, ordered_ref, other_ref, logits_ref, 0)
+    for copy in fetches[now:]:
         copy.wait()
-    scores(2)
-    rest(1)
-    scores(3)
-    rest(2)
-    rest(3)
-
-
-def sums_kernel(tokens_ref, logits_ref, mine_ref, combine_ref):
+
+
+def last_scores_kernel(tokens_ref, ordered_ref, other_ref, logits_ref):
+    scores(tokens_ref, ordered_ref, other_ref, logits_ref, tokens_ref.shape[0] - logits_ref.shape[0])
+
+
+def sums_kernel(tokens_ref, first_ref, last_ref, mine_ref, combine_ref):
     half = mine_ref.shape[1]
+    now = first_ref.shape[0]
     for c in range(tokens_ref.shape[0]):
-        logits = logits_ref[c]
+        logits = first_ref[c] if c < now else last_ref[c - now]
         store_sums(mine_ref, c, *stats_columns(logits[:, :half]), tokens_ref[c])
         exponent = jnp.exp(logits - jnp.max(logits, axis=1, keepdims=True))
         combine_ref[c] = (exponent * (1.0 / jnp.sum(exponent, axis=1, keepdims=True))).astype(BF16)
 
 
-def merge_kernel(mine_ref, theirs_ref, out_ref):
+def merge_kernel(mine_ref, first_ref, last_ref, out_ref):
     clips, half, width = mine_ref.shape
     depth = width - STAT
     rows, part = 256, 256 // clips
@@ -110,15 +116,15 @@
         at = slice(group * part, group * part + part)
         to = slice(group * rows // 8, (group + 1) * rows // 8)
 
-        def load(ref, lo, hi):
-            return ref[:, at, lo:hi].astype(F32).reshape(rows, hi - lo)
+        def load(lo, hi, *refs):
+            return jnp.concatenate([ref[:, at, lo:hi] for ref in refs]).astype(F32).reshape(rows, hi - lo)
 
         def store(lo, hi, value):
             moved = jnp.dot(order, value.astype(BF16), preferred_element_type=F32)
             out_ref[to, :, lo:hi] = moved.reshape(rows // 8, 8, hi - lo).astype(BF16)
 
-        top_a, total_a = read_stats(load(mine_ref, depth, width))
-        top_b, total_b = read_stats(load(theirs_ref, depth, width))
+        top_a, total_a = read_stats(load(depth, width, mine_ref))
+        top_b, total_b = read_stats(load(depth, width, first_ref, last_ref))
         top = jnp.maximum(top_a, top_b)
         weight_a = total_a * jnp.exp(top_a - top)
         weight_b = total_b * jnp.exp(top_b - top)
@@ -132,7 +138,7 @@
         weight_a, weight_b = weight_a * inverse, weight_b * inverse
         for lo in range(0, depth, 256):
             hi = lo + 256
-            store(lo, hi, load(mine_ref, lo, hi) * weight_a + load(theirs_ref, lo, hi) * weight_b)
+            store(lo, hi, load(lo, hi, mine_ref) * weight_a + load(lo, hi, first_ref, last_ref) * weight_b)
 
 
 def expert_kernel(tile, received_ref, up_ref, down_ref, out_ref, rows_ref, hidden_ref):
@@ -190,6 +196,10 @@
         copy.wait()
 
 
+def in_hbm(array):
+    return pltpu.with_memory_space_constraint(array, pltpu.HBM)
+
+
 def params(mib):
     return pltpu.CompilerParams(vmem_limit_bytes=mib * MIB)
 
@@ -206,39 +216,54 @@
     whole = pl.BlockSpec(memory_space=pltpu.VMEM)
     far = pl.BlockSpec(memory_space=pltpu.HBM)
 
-    other, near, logits = pl.pallas_call(
-        scores_kernel,
-        in_specs=[pl.BlockSpec(memory_space=pltpu.SMEM), far, whole],
-        out_specs=[whole] * 3,
-        out_shape=[
-            jax.ShapeDtypeStruct((clips, half, wide), BF16),
-            jax.ShapeDtypeStruct((clips, count, depth), BF16),
-            jax.ShapeDtypeStruct((clips, count, slots), F32),
-        ],
-        scratch_shapes=[pltpu.VMEM((depth, slots), BF16), pltpu.SemaphoreType.DMA((clips,))],
-        compiler_params=params(39),
-    )(core, tokens, router)
-
-    theirs = lax.ppermute(other, "core", swap)
+    now = 2
+    near_shape = jax.ShapeDtypeStruct((clips, count, depth), BF16)
+    ordered_shape = jax.ShapeDtypeStruct((depth, slots), BF16)
+
+    def part(amount):
+        return [
+            jax.ShapeDtypeStruct((amount, half, wide), BF16),
+            jax.ShapeDtypeStruct((amount, count, slots), F32),
+        ]
+
+    other, logits = part(now)
+    first_other, near, first_logits, ordered = pl.pallas_call(
+        first_scores_kernel,
+        in_specs=[pl.BlockSpec(memory_space=pltpu.SMEM), far, far],
+        out_specs=[whole] * 4,
+        out_shape=[other, near_shape, logits, ordered_shape],
+        scratch_shapes=[pltpu.VMEM((depth, slots), BF16), pltpu.SemaphoreType.DMA((clips + 1,))],
+        compiler_params=params(36),
+    )(core, in_hbm(tokens), in_hbm(router))
+    first_theirs = lax.ppermute(first_other, "core", swap)
+
+    last_other, last_logits = pl.pallas_call(
+        last_scores_kernel,
+        in_specs=[whole] * 2,
+        out_specs=[whole] * 2,
+        out_shape=part(clips - now),
+        compiler_params=params(16),
+    )(near, ordered)
+    last_theirs = lax.ppermute(last_other, "core", swap)
 
     mine, combine = pl.pallas_call(
         sums_kernel,
-        in_specs=[whole] * 2,
+        in_specs=[whole] * 3,
         out_specs=[whole] * 2,
         out_shape=[
             jax.ShapeDtypeStruct((clips, half, wide), BF16),
             jax.ShapeDtypeStruct((clips, count, slots), BF16),
         ],
         compiler_params=params(16),
-    )(near, logits)
+    )(near, first_logits, last_logits)
 
     merged = pl.pallas_call(
         merge_kernel,
-        in_specs=[whole] * 2,
+        in_specs=[whole] * 3,
         out_specs=whole,
         out_shape=jax.ShapeDtypeStruct((CHIPS, 8, wide), BF16),
         compiler_params=params(16),
-    )(mine, theirs)
+    )(mine, first_theirs, last_theirs)
 
     received = lax.all_to_all(merged, chips, 0, 0, tiled=False)
 

time: 82 us -> 80.3 us (0.979)
  local copies, waits for them, and re-layouts: 1.1 us -> 0.01 us
    unnamed x10 -> x8, local copies, waits for them, and re-layouts: 1.1 us -> 0.01 us
    pallas_call x3 -> x4, Pallas kernels: 9.18 us -> 9.1 us  [the longest x1 4.14 us: shards(): pl.pallas_call(first_scores_kernel, in_specs=[pl.BlockSpec(memory_space=p...]
  transfers between devices with their start and end apart: 2 -> 3, of which waited for: 2 -> 2; matrix products, arithmetic and copies ran while one was open for 0% -> 0% of each run, Pallas kernels for 3% -> 5%
where the time goes in v4:
time: 80.3 us; the launch traced here: 80.1 us
  blocking collectives  56.2 us (70%)
  Pallas kernels  15.5 us (19%)
  starting transfers between devices  5.59 us (7%)
  waiting for transfers between devices  2.55 us (3%)
    all_to_all x1, blocking collectives, shards(): received = lax.all_to_all(merged, chips, 0, 0, tiled=False)  32.3 us
    all_to_all x1, blocking collectives, shards(): returned = lax.all_to_all(results, chips, 0, 0, tiled=False)  23.9 us
    pallas_call x1, Pallas kernels, shards(): pl.pallas_call(first_scores_kernel, in_specs=[pl.BlockSpec(memory_space=p...  4.14 us
    ppermute x1, starting transfers between devices, shards(): partner = lax.ppermute(returned, 'core', swap)  3.95 us
    pallas_call x1, Pallas kernels, shards(): pl.pallas_call(functools.partial(mix_kernel, tile), in_specs=[whole] * 3,...  3.59 us
    pallas_call x1, Pallas kernels, shards(): pl.pallas_call(functools.partial(expert_kernel, 256), in_specs=[whole] *...  2.35 us
    ppermute x1, waiting for transfers between devices, shards(): partner = lax.ppermute(returned, 'core', swap)  2.15 us
    pallas_call x1, Pallas kernels, shards(): pl.pallas_call(last_scores_kernel, in_specs=[whole] * 2, out_specs=[whole...  1.82 us
  transfers between devices with their start and end apart: 3, of which 2 were waited for; matrix products, arithmetic and copies ran while one was open for 0% of the time, Pallas kernels for 5%

profile of v4, /device:TPU:1, one launch (start us, length us, event | category | flops | bytes accessed | tf_op | source)
XLA Modules:
  0.0 80.1 jit_solution(14010216271107909191)
XLA Ops:
  0.0 4.1 %shard_map.46 = (bf16[2,128,1408]{2,1,0:T(8,128)(2,1)S(1)}, bf16[4,640,1280]{2,1,0:T(8,128)(2,1)S(1)}, f32[2,640,256]{2,1,0:T(8,128)S(1)}, bf16[1280,256]{1,0:T(8,128)(2,1)S(1)}) custom-call(s32[1]{0:T(128)} %bitcast.core_ref, bf16[4,640,1280]{2,1,0:T(8,128)(2,1)} %tokens_hbm.1, bf16[1280,256]{1,0:T(8,128)(2,1)} %router_hbm.1), custom_call_target="tpu_custom_call" | custom-call | tf_op jit(solution)/shard_map/pallas_call | solution.py:230
  4.1 1.5 %collective-permute-start = (bf16[2,128,1408]{2,1,0:T(8,128)(2,1)S(1)}, bf16[2,128,1408]{2,1,0:T(8,128)(2,1)S(1)}, u32[]{:S(2)}, u32[]{:S(2)}) collective-permute-start(bf16[2,128,1408]{2,1,0:T(8,128)(2,1)S(1)} %get-tuple-element.18), channel_id=1, source_target_pairs={{0,1},{1,0},{2,3},{3,2},{4,5},{5,4},{6,7},{7,6},{8,9},{9,8},{10,11... | collective-permute-start | bytes 2162696 | tf_op jit(solution)/shard_map/ppermute | solution.py:238
  5.6 0.0 slice-start
  5.7 0.0 slice-start.2
  5.7 1.8 %shard_map.47 = (bf16[2,128,1408]{2,1,0:T(8,128)(2,1)S(1)}, f32[2,640,256]{2,1,0:T(8,128)S(1)}) custom-call(bf16[4,640,1280]{2,1,0:T(8,128)(2,1)S(1)} %get-tuple-element.13.tokens_ref, bf16[1280,256]{1,0:T(8,128)(2,1)S(1)} %get-tuple-element.15.ordered_ref), custom_call_target="tpu_custom_call" | custom-call | tf_op jit(solution)/shard_map/pallas_call | solution.py:240
  7.5 0.1 collective-permute-start.1
  7.6 0.0 slice-start.1
  7.6 0.0 slice-start.3
  7.6 1.7 %shard_map.48 = (bf16[4,128,1408]{2,1,0:T(8,128)(2,1)S(1)}, bf16[4,640,256]{2,1,0:T(8,128)(2,1)S(1)}) custom-call(bf16[4,640,1280]{2,1,0:T(8,128)(2,1)S(1)} %get-tuple-element.13.tokens_ref, f32[2,640,256]{2,1,0:T(8,128)S(1)} %get-tuple-element.14.first_ref, f32[2,640,256]{2,1,0:T(8,128)S(1)} %get-tuple-element.16.last_ref), custom_call_target="tpu_custom_call" | custom-call | tf_op jit(solution)/shard_map/pallas_call | solution.py:249
  9.3 0.0 collective-permute-done.first_ref
  9.4 0.4 collective-permute-done.1.last_ref
  9.8 1.4 %shard_map.49 = bf16[64,8,1408]{2,1,0:T(8,128)(2,1)S(1)} custom-call(bf16[4,128,1408]{2,1,0:T(8,128)(2,1)S(1)} %get-tuple-element.17.mine_ref, bf16[2,128,1408]{2,1,0:T(8,128)(2,1)S(1)} %collective-permute-done.first_ref, bf16[2,128,1408]{2,1,0:T(8,128)(2,1)S(1)} %collective-permute-done.1.last_ref), custom_call_target="tpu_custom_call" | custom-call | tf_op jit(solution)/shard_map/pallas_call | solution.py:260
  11.2 32.3 %all_to_all.10.received_ref = bf16[64,8,1408]{2,1,0:T(8,128)(2,1)S(1)} all-to-all(bf16[64,8,1408]{2,1,0:T(8,128)(2,1)S(1)} %shard_map.49), channel_id=1, replica_groups=mesh['x'=4,'z'=4,'y'=4,'core'=2] {'x','z','y'}, dimensions={0} | all-to-all | bytes 2883584 | tf_op jit(solution)/shard_map/all_to_all | solution.py:268
  43.5 0.0 slice-done
  43.5 0.0 slice-done.2
  43.5 0.0 slice-done.1
  43.5 0.0 slice-done.3
  43.5 2.4 %shard_map.50 = bf16[64,8,1280]{2,1,0:T(8,128)(2,1)S(1)} custom-call(bf16[64,8,1408]{2,1,0:T(8,128)(2,1)S(1)} %all_to_all.10.received_ref, bf16[1,1280,2560]{2,1,0:T(8,128)(2,1)S(1)} %bitcast.2, bf16[1,2560,1280]{2,1,0:T(8,128)(2,1)S(1)} %bitcast.4), custom_call_target="tpu_custom_call" | custom-call | tf_op jit(solution)/shard_map/pallas_call | solution.py:270
  45.9 23.9 %all_to_all.11.ref = bf16[64,8,1280]{2,1,0:T(8,128)(2,1)S(1)} all-to-all(bf16[64,8,1280]{2,1,0:T(8,128)(2,1)S(1)} %shard_map.50), channel_id=1, replica_groups=mesh['x'=4,'z'=4,'y'=4,'core'=2] {'x','z','y'}, dimensions={0} | all-to-all | bytes 2621440 | tf_op jit(solution)/shard_map/all_to_all | solution.py:279
  69.7 4.0 %collective-permute-start.2 = (bf16[64,8,1280]{2,1,0:T(8,128)(2,1)S(1)}, bf16[64,8,1280]{2,1,0:T(8,128)(2,1)S(1)}, u32[]{:S(2)}, u32[]{:S(2)}) collective-permute-start(bf16[64,8,1280]{2,1,0:T(8,128)(2,1)S(1)} %all_to_all.11.ref), channel_id=1, source_target_pairs={{0,1},{1,0},{2,3},{3,2},{4,5},{5,4},{6,7},{7,6},{8,9},{9,8},{10,11... | collective-permute-start | bytes 3932168 | tf_op jit(solution)/shard_map/ppermute | solution.py:280
  73.7 0.5 shard_map.51.mine_ref
  74.2 2.1 %collective-permute-done.2.theirs_ref = bf16[64,8,1280]{2,1,0:T(8,128)(2,1)S(1)} collective-permute-done((bf16[64,8,1280]{2,1,0:T(8,128)(2,1)S(1)}, bf16[64,8,1280]{2,1,0:T(8,128)(2,1)S(1)}, u32[]{:S(2)}, u32[]{:S(2)}) %collective-permute-start.2) | collective-permute-done | bytes 1310752 | tf_op jit(solution)/shard_map/ppermute | solution.py:280
  76.4 3.6 %shard_map.52 = bf16[4,640,1280]{2,1,0:T(8,128)(2,1)} custom-call(bf16[4,128,1280]{2,1,0:T(8,128)(2,1)S(1)} %shard_map.51.mine_ref, bf16[64,8,1280]{2,1,0:T(8,128)(2,1)S(1)} %collective-permute-done.2.theirs_ref, bf16[4,640,256]{2,1,0:T(8,128)(2,1)S(1)} %get-tuple-element.20.combine_ref), custom_call_target="tpu_custom_call" | custom-call | tf_op jit(solution)/shard_map/pallas_call | solution.py:291
  (2 shorter events, 0.0 us)
Async XLA Ops:
  4.1 5.2 %collective-permute-start = (bf16[2,128,1408]{2,1,0:T(8,128)(2,1)S(1)}, bf16[2,128,1408]{2,1,0:T(8,128)(2,1)S(1)}, u32[]{:S(2)}, u32[]{:S(2)}) collective-permute-start(bf16[2,128,1408]{2,1,0:T(8,128)(2,1)S(1)} %get-tuple-element.18), channel_id=1, source_target_pairs={{0,1},{1,0},{2,3},{3,2},{4,5},{5,4},{6,7},{7,6},{8,9},{9,8},{10,11... | collective-permute-start | bytes 2162696 | tf_op jit(solution)/shard_map/ppermute | solution.py:238
  5.6 37.8 %slice-start = ((s8[6553600]{0:T(1024)(128)(4,1)}), s8[4194304]{0:T(1024)(128)(4,1)S(1)}, s32[]{:S(2)}) async-start(s8[6553600]{0:T(1024)(128)(4,1)} %bitcast.1), calls=%async_computation.2 | async-start | bytes 8388608
  5.7 37.8 %slice-start.2 = ((s8[6553600]{0:T(1024)(128)(4,1)}), s8[4194304]{0:T(1024)(128)(4,1)S(1)}, s32[]{:S(2)}) async-start(s8[6553600]{0:T(1024)(128)(4,1)} %bitcast.3), calls=%async_computation.4 | async-start | bytes 8388608
  7.5 2.3 %collective-permute-start.1 = (bf16[2,128,1408]{2,1,0:T(8,128)(2,1)S(1)}, bf16[2,128,1408]{2,1,0:T(8,128)(2,1)S(1)}, u32[]{:S(2)}, u32[]{:S(2)}) collective-permute-start(bf16[2,128,1408]{2,1,0:T(8,128)(2,1)S(1)} %get-tuple-element.19), channel_id=1, source_target_pairs={{0,1},{1,0},{2,3},{3,2},{4,5},{5,4},{6,7},{7,6},{8,9},{9,8},{10,11... | collective-permute-start | bytes 2162696 | tf_op jit(solution)/shard_map/ppermute | solution.py:247
  7.6 35.9 %slice-start.1 = ((s8[6553600]{0:T(1024)(128)(4,1)}), s8[2359296]{0:T(1024)(128)(4,1)S(1)}, s32[]{:S(2)}) async-start(s8[6553600]{0:T(1024)(128)(4,1)} %bitcast.1), calls=%async_computation.3 | async-start | bytes 4718592
  7.6 35.9 %slice-start.3 = ((s8[6553600]{0:T(1024)(128)(4,1)}), s8[2359296]{0:T(1024)(128)(4,1)S(1)}, s32[]{:S(2)}) async-start(s8[6553600]{0:T(1024)(128)(4,1)} %bitcast.3), calls=%async_computation.5 | async-start | bytes 4718592
  69.7 6.6 %collective-permute-start.2 = (bf16[64,8,1280]{2,1,0:T(8,128)(2,1)S(1)}, bf16[64,8,1280]{2,1,0:T(8,128)(2,1)S(1)}, u32[]{:S(2)}, u32[]{:S(2)}) collective-permute-start(bf16[64,8,1280]{2,1,0:T(8,128)(2,1)S(1)} %all_to_all.11.ref), channel_id=1, source_target_pairs={{0,1},{1,0},{2,3},{3,2},{4,5},{5,4},{6,7},{7,6},{8,9},{9,8},{10,11... | collective-permute-start | bytes 3932168 | tf_op jit(solution)/shard_map/ppermute | solution.py:280

commit v5 on v4

--- a/solution.py
+++ b/solution.py
@@ -97,14 +97,12 @@
     scores(tokens_ref, ordered_ref, other_ref, logits_ref, tokens_ref.shape[0] - logits_ref.shape[0])
 
 
-def sums_kernel(tokens_ref, first_ref, last_ref, mine_ref, combine_ref):
+def sums_kernel(tokens_ref, first_ref, last_ref, mine_ref):
     half = mine_ref.shape[1]
     now = first_ref.shape[0]
     for c in range(tokens_ref.shape[0]):
-        logits = first_ref[c] if c < now else last_ref[c - now]
-        store_sums(mine_ref, c, *stats_columns(logits[:, :half]), tokens_ref[c])
-        exponent = jnp.exp(logits - jnp.max(logits, axis=1, keepdims=True))
-        combine_ref[c] = (exponent * (1.0 / jnp.sum(exponent, axis=1, keepdims=True))).astype(BF16)
+        logits = first_ref[c, :, :half] if c < now else last_ref[c - now, :, :half]
+        store_sums(mine_ref, c, *stats_columns(logits), tokens_ref[c])
 
 
 def merge_kernel(mine_ref, first_ref, last_ref, out_ref):
@@ -179,6 +177,15 @@
             out_ref[:, group * part:group * part + part, lo:lo + 256] = moved.reshape(clips, part, 256)
 
 
+def window_kernel(mine_ref, first_ref, last_ref, slots_ref, combine_ref):
+    by_clip(mine_ref, slots_ref)
+    now = first_ref.shape[0]
+    for c in range(combine_ref.shape[0]):
+        logits = first_ref[c] if c < now else last_ref[c - now]
+        exponent = jnp.exp(logits - jnp.max(logits, axis=1, keepdims=True))
+        combine_ref[c] = (exponent * (1.0 / jnp.sum(exponent, axis=1, keepdims=True))).astype(BF16)
+
+
 def mix_kernel(tile, mine_ref, theirs_ref, combine_ref, out_hbm, slots_ref, out_ref, sems):
     by_clip(theirs_ref, slots_ref)
     copies = []
@@ -246,14 +253,11 @@
     )(near, ordered)
     last_theirs = lax.ppermute(last_other, "core", swap)
 
-    mine, combine = pl.pallas_call(
+    mine = pl.pallas_call(
         sums_kernel,
         in_specs=[whole] * 3,
-        out_specs=[whole] * 2,
-        out_shape=[
-            jax.ShapeDtypeStruct((clips, half, wide), BF16),
-            jax.ShapeDtypeStruct((clips, count, slots), BF16),
-        ],
+        out_specs=whole,
+        out_shape=jax.ShapeDtypeStruct((clips, half, wide), BF16),
         compiler_params=params(16),
     )(near, first_logits, last_logits)
 
@@ -279,15 +283,18 @@
     returned = lax.all_to_all(results, chips, 0, 0, tiled=False)
     partner = lax.ppermute(returned, "core", swap)
 
-    own = pl.pallas_call(
-        by_clip,
-        in_specs=[whole],
-        out_specs=whole,
-        out_shape=jax.ShapeDtypeStruct((clips, half, depth), BF16),
+    own, combine = pl.pallas_call(
+        window_kernel,
+        in_specs=[whole] * 3,
+        out_specs=[whole] * 2,
+        out_shape=[
+            jax.ShapeDtypeStruct((clips, half, depth), BF16),
+            jax.ShapeDtypeStruct((clips, count, slots), BF16),
+        ],
         compiler_params=params(16),
-    )(returned)
-
-    tile = count // 2
+    )(returned, first_logits, last_logits)
+
+    tile = count // 4
     return pl.pallas_call(
         functools.partial(mix_kernel, tile),
         in_specs=[whole] * 3,
@@ -296,7 +303,7 @@
         scratch_shapes=[
             pltpu.VMEM((clips, half, depth), BF16),
             pltpu.VMEM((clips, count, depth), BF16),
-            pltpu.SemaphoreType.DMA((clips * 2,)),
+            pltpu.SemaphoreType.DMA((clips * 4,)),
         ],
         compiler_params=params(24),
     )(own, partner, combine)

time: 80.3 us -> 80.2 us (level)
  no operation moved by 1% of the time
where the time goes in v5:
time: 80.2 us; the launch traced here: 80.1 us
  blocking collectives  56.2 us (70%)
  Pallas kernels  15.7 us (20%)
  starting transfers between devices  5.58 us (7%)
  waiting for transfers between devices  2.38 us (3%)
    all_to_all x1, blocking collectives, shards(): received = lax.all_to_all(merged, chips, 0, 0, tiled=False)  32.3 us
    all_to_all x1, blocking collectives, shards(): returned = lax.all_to_all(results, chips, 0, 0, tiled=False)  23.9 us
    pallas_call x1, Pallas kernels, shards(): pl.pallas_call(first_scores_kernel, in_specs=[pl.BlockSpec(memory_space=p...  4.15 us
    ppermute x1, starting transfers between devices, shards(): partner = lax.ppermute(returned, 'core', swap)  3.96 us
    pallas_call x1, Pallas kernels, shards(): pl.pallas_call(functools.partial(mix_kernel, tile), in_specs=[whole] * 3,...  3.51 us
    pallas_call x1, Pallas kernels, shards(): pl.pallas_call(functools.partial(expert_kernel, 256), in_specs=[whole] *...  2.35 us
    pallas_call x1, Pallas kernels, shards(): pl.pallas_call(last_scores_kernel, in_specs=[whole] * 2, out_specs=[whole...  1.84 us
    ppermute x1, waiting for transfers between devices, shards(): partner = lax.ppermute(returned, 'core', swap)  1.78 us
  transfers between devices with their start and end apart: 3, of which 2 were waited for; matrix products, arithmetic and copies ran while one was open for 0% of the time, Pallas kernels for 5%

profile of v5, /device:TPU:1, one launch (start us, length us, event | category | flops | bytes accessed | tf_op | source)
XLA Modules:
  0.0 80.1 jit_solution(6035536171251650762)
XLA Ops:
  0.0 4.1 %shard_map.46 = (bf16[2,128,1408]{2,1,0:T(8,128)(2,1)S(1)}, bf16[4,640,1280]{2,1,0:T(8,128)(2,1)S(1)}, f32[2,640,256]{2,1,0:T(8,128)S(1)}, bf16[1280,256]{1,0:T(8,128)(2,1)S(1)}) custom-call(s32[1]{0:T(128)} %bitcast.core_ref, bf16[4,640,1280]{2,1,0:T(8,128)(2,1)} %tokens_hbm.1, bf16[1280,256]{1,0:T(8,128)(2,1)} %router_hbm.1), custom_call_target="tpu_custom_call" | custom-call | tf_op jit(solution)/shard_map/pallas_call | solution.py:237
  4.2 1.5 %collective-permute-start = (bf16[2,128,1408]{2,1,0:T(8,128)(2,1)S(1)}, bf16[2,128,1408]{2,1,0:T(8,128)(2,1)S(1)}, u32[]{:S(2)}, u32[]{:S(2)}) collective-permute-start(bf16[2,128,1408]{2,1,0:T(8,128)(2,1)S(1)} %get-tuple-element.17), channel_id=1, source_target_pairs={{0,1},{1,0},{2,3},{3,2},{4,5},{5,4},{6,7},{7,6},{8,9},{9,8},{10,11... | collective-permute-start | bytes 2162696 | tf_op jit(solution)/shard_map/ppermute | solution.py:245
  5.7 0.0 slice-start
  5.7 0.0 slice-start.2
  5.7 1.8 %shard_map.47 = (bf16[2,128,1408]{2,1,0:T(8,128)(2,1)S(1)}, f32[2,640,256]{2,1,0:T(8,128)S(1)}) custom-call(bf16[4,640,1280]{2,1,0:T(8,128)(2,1)S(1)} %get-tuple-element.13.tokens_ref, bf16[1280,256]{1,0:T(8,128)(2,1)S(1)} %get-tuple-element.15.ordered_ref), custom_call_target="tpu_custom_call" | custom-call | tf_op jit(solution)/shard_map/pallas_call | solution.py:247
  7.5 0.1 collective-permute-start.1
  7.6 0.0 slice-start.1
  7.6 0.0 slice-start.3
  7.6 1.5 %shard_map.48.mine_ref = bf16[4,128,1408]{2,1,0:T(8,128)(2,1)S(1)} custom-call(bf16[4,640,1280]{2,1,0:T(8,128)(2,1)S(1)} %get-tuple-element.13.tokens_ref, f32[2,640,256]{2,1,0:T(8,128)S(1)} %get-tuple-element.14.first_ref, f32[2,640,256]{2,1,0:T(8,128)S(1)} %get-tuple-element.16.last_ref), custom_call_target="tpu_custom_call" | custom-call | tf_op jit(solution)/shard_map/pallas_call | solution.py:256
  9.2 0.0 collective-permute-done.first_ref
  9.2 0.6 collective-permute-done.1.last_ref
  9.8 1.4 %shard_map.49 = bf16[64,8,1408]{2,1,0:T(8,128)(2,1)S(1)} custom-call(bf16[4,128,1408]{2,1,0:T(8,128)(2,1)S(1)} %shard_map.48.mine_ref, bf16[2,128,1408]{2,1,0:T(8,128)(2,1)S(1)} %collective-permute-done.first_ref, bf16[2,128,1408]{2,1,0:T(8,128)(2,1)S(1)} %collective-permute-done.1.last_ref), custom_call_target="tpu_custom_call" | custom-call | tf_op jit(solution)/shard_map/pallas_call | solution.py:264
  11.2 32.3 %all_to_all.10.received_ref = bf16[64,8,1408]{2,1,0:T(8,128)(2,1)S(1)} all-to-all(bf16[64,8,1408]{2,1,0:T(8,128)(2,1)S(1)} %shard_map.49), channel_id=1, replica_groups=mesh['x'=4,'z'=4,'y'=4,'core'=2] {'x','z','y'}, dimensions={0} | all-to-all | bytes 2883584 | tf_op jit(solution)/shard_map/all_to_all | solution.py:272
  43.5 0.0 slice-done
  43.5 0.0 slice-done.2
  43.5 0.0 slice-done.1
  43.5 0.0 slice-done.3
  43.6 2.4 %shard_map.50 = bf16[64,8,1280]{2,1,0:T(8,128)(2,1)S(1)} custom-call(bf16[64,8,1408]{2,1,0:T(8,128)(2,1)S(1)} %all_to_all.10.received_ref, bf16[1,1280,2560]{2,1,0:T(8,128)(2,1)S(1)} %bitcast.2, bf16[1,2560,1280]{2,1,0:T(8,128)(2,1)S(1)} %bitcast.4), custom_call_target="tpu_custom_call" | custom-call | tf_op jit(solution)/shard_map/pallas_call | solution.py:274
  45.9 23.9 %all_to_all.11.mine_ref = bf16[64,8,1280]{2,1,0:T(8,128)(2,1)S(1)} all-to-all(bf16[64,8,1280]{2,1,0:T(8,128)(2,1)S(1)} %shard_map.50), channel_id=1, replica_groups=mesh['x'=4,'z'=4,'y'=4,'core'=2] {'x','z','y'}, dimensions={0} | all-to-all | bytes 2621440 | tf_op jit(solution)/shard_map/all_to_all | solution.py:283
  69.8 4.0 %collective-permute-start.2 = (bf16[64,8,1280]{2,1,0:T(8,128)(2,1)S(1)}, bf16[64,8,1280]{2,1,0:T(8,128)(2,1)S(1)}, u32[]{:S(2)}, u32[]{:S(2)}) collective-permute-start(bf16[64,8,1280]{2,1,0:T(8,128)(2,1)S(1)} %all_to_all.11.mine_ref), channel_id=1, source_target_pairs={{0,1},{1,0},{2,3},{3,2},{4,5},{5,4},{6,7},{7,6},{8,9},{9,8},{10,11... | collective-permute-start | bytes 3932168 | tf_op jit(solution)/shard_map/ppermute | solution.py:284
  73.7 0.9 %shard_map.51 = (bf16[4,128,1280]{2,1,0:T(8,128)(2,1)S(1)}, bf16[4,640,256]{2,1,0:T(8,128)(2,1)S(1)}) custom-call(bf16[64,8,1280]{2,1,0:T(8,128)(2,1)S(1)} %all_to_all.11.mine_ref, f32[2,640,256]{2,1,0:T(8,128)S(1)} %get-tuple-element.14.first_ref, f32[2,640,256]{2,1,0:T(8,128)S(1)} %get-tuple-element.16.last_ref), custom_call_target="tpu_custom_call" | custom-call | tf_op jit(solution)/shard_map/pallas_call | solution.py:286
  74.6 1.8 %collective-permute-done.2.theirs_ref = bf16[64,8,1280]{2,1,0:T(8,128)(2,1)S(1)} collective-permute-done((bf16[64,8,1280]{2,1,0:T(8,128)(2,1)S(1)}, bf16[64,8,1280]{2,1,0:T(8,128)(2,1)S(1)}, u32[]{:S(2)}, u32[]{:S(2)}) %collective-permute-start.2) | collective-permute-done | bytes 1310752 | tf_op jit(solution)/shard_map/ppermute | solution.py:284
  76.4 3.5 %shard_map.52 = bf16[4,640,1280]{2,1,0:T(8,128)(2,1)} custom-call(bf16[4,128,1280]{2,1,0:T(8,128)(2,1)S(1)} %get-tuple-element.19.mine_ref, bf16[64,8,1280]{2,1,0:T(8,128)(2,1)S(1)} %collective-permute-done.2.theirs_ref, bf16[4,640,256]{2,1,0:T(8,128)(2,1)S(1)} %get-tuple-element.20.combine_ref), custom_call_target="tpu_custom_call" | custom-call | tf_op jit(solution)/shard_map/pallas_call | solution.py:298
  (2 shorter events, 0.0 us)
Async XLA Ops:
  4.2 5.0 %collective-permute-start = (bf16[2,128,1408]{2,1,0:T(8,128)(2,1)S(1)}, bf16[2,128,1408]{2,1,0:T(8,128)(2,1)S(1)}, u32[]{:S(2)}, u32[]{:S(2)}) collective-permute-start(bf16[2,128,1408]{2,1,0:T(8,128)(2,1)S(1)} %get-tuple-element.17), channel_id=1, source_target_pairs={{0,1},{1,0},{2,3},{3,2},{4,5},{5,4},{6,7},{7,6},{8,9},{9,8},{10,11... | collective-permute-start | bytes 2162696 | tf_op jit(solution)/shard_map/ppermute | solution.py:245
  5.7 37.9 %slice-start = ((s8[6553600]{0:T(1024)(128)(4,1)}), s8[4194304]{0:T(1024)(128)(4,1)S(1)}, s32[]{:S(2)}) async-start(s8[6553600]{0:T(1024)(128)(4,1)} %bitcast.1), calls=%async_computation.2 | async-start | bytes 8388608
  5.7 37.9 %slice-start.2 = ((s8[6553600]{0:T(1024)(128)(4,1)}), s8[4194304]{0:T(1024)(128)(4,1)S(1)}, s32[]{:S(2)}) async-start(s8[6553600]{0:T(1024)(128)(4,1)} %bitcast.3), calls=%async_computation.4 | async-start | bytes 8388608
  7.5 2.3 %collective-permute-start.1 = (bf16[2,128,1408]{2,1,0:T(8,128)(2,1)S(1)}, bf16[2,128,1408]{2,1,0:T(8,128)(2,1)S(1)}, u32[]{:S(2)}, u32[]{:S(2)}) collective-permute-start(bf16[2,128,1408]{2,1,0:T(8,128)(2,1)S(1)} %get-tuple-element.18), channel_id=1, source_target_pairs={{0,1},{1,0},{2,3},{3,2},{4,5},{5,4},{6,7},{7,6},{8,9},{9,8},{10,11... | collective-permute-start | bytes 2162696 | tf_op jit(solution)/shard_map/ppermute | solution.py:254
  7.6 35.9 %slice-start.1 = ((s8[6553600]{0:T(1024)(128)(4,1)}), s8[2359296]{0:T(1024)(128)(4,1)S(1)}, s32[]{:S(2)}) async-start(s8[6553600]{0:T(1024)(128)(4,1)} %bitcast.1), calls=%async_computation.3 | async-start | bytes 4718592
  7.6 35.9 %slice-start.3 = ((s8[6553600]{0:T(1024)(128)(4,1)}), s8[2359296]{0:T(1024)(128)(4,1)S(1)}, s32[]{:S(2)}) async-start(s8[6553600]{0:T(1024)(128)(4,1)} %bitcast.3), calls=%async_computation.5 | async-start | bytes 4718592
  69.8 6.6 %collective-permute-start.2 = (bf16[64,8,1280]{2,1,0:T(8,128)(2,1)S(1)}, bf16[64,8,1280]{2,1,0:T(8,128)(2,1)S(1)}, u32[]{:S(2)}, u32[]{:S(2)}) collective-permute-start(bf16[64,8,1280]{2,1,0:T(8,128)(2,1)S(1)} %all_to_all.11.mine_ref), channel_id=1, source_target_pairs={{0,1},{1,0},{2,3},{3,2},{4,5},{5,4},{6,7},{7,6},{8,9},{9,8},{10,11... | collective-permute-start | bytes 3932168 | tf_op jit(solution)/shard_map/ppermute | solution.py:284

commit v6 on v4

--- a/solution.py
+++ b/solution.py
@@ -83,11 +83,11 @@
     source = within // 2 * 4 + owner * 2 + within % 2
     chosen = jnp.where(row == source, 1.0, 0.0).astype(BF16)
     fetch.wait()
-    for copy in fetches[now:]:
-        copy.start()
     ordered_ref[...] = jnp.dot(router_ref[...], chosen, preferred_element_type=F32).astype(BF16)
     for copy in fetches[:now]:
         copy.wait()
+    for copy in fetches[now:]:
+        copy.start()
     scores(tokens_ref, ordered_ref, other_ref, logits_ref, 0)
     for copy in fetches[now:]:
         copy.wait()

time: 80.3 us -> 80.3 us (level)
  no operation moved by 1% of the time
where the time goes in v6:
time: 80.3 us; the launch traced here: 80.1 us
  blocking collectives  56.2 us (70%)
  Pallas kernels  15.5 us (19%)
  starting transfers between devices  5.59 us (7%)
  waiting for transfers between devices  2.55 us (3%)
    all_to_all x1, blocking collectives, shards(): received = lax.all_to_all(merged, chips, 0, 0, tiled=False)  32.3 us
    all_to_all x1, blocking collectives, shards(): returned = lax.all_to_all(results, chips, 0, 0, tiled=False)  23.9 us
    pallas_call x1, Pallas kernels, shards(): pl.pallas_call(first_scores_kernel, in_specs=[pl.BlockSpec(memory_space=p...  4.14 us
    ppermute x1, starting transfers between devices, shards(): partner = lax.ppermute(returned, 'core', swap)  3.95 us
    pallas_call x1, Pallas kernels, shards(): pl.pallas_call(functools.partial(mix_kernel, tile), in_specs=[whole] * 3,...  3.59 us
    pallas_call x1, Pallas kernels, shards(): pl.pallas_call(functools.partial(expert_kernel, 256), in_specs=[whole] *...  2.35 us
    ppermute x1, waiting for transfers between devices, shards(): partner = lax.ppermute(returned, 'core', swap)  2.15 us
    pallas_call x1, Pallas kernels, shards(): pl.pallas_call(last_scores_kernel, in_specs=[whole] * 2, out_specs=[whole...  1.82 us
  transfers between devices with their start and end apart: 3, of which 2 were waited for; matrix products, arithmetic and copies ran while one was open for 0% of the time, Pallas kernels for 5%

profile of v6, /device:TPU:1, one launch (start us, length us, event | category | flops | bytes accessed | tf_op | source)
XLA Modules:
  0.0 80.1 jit_solution(12454407099464176983)
XLA Ops:
  0.0 4.1 %shard_map.46 = (bf16[2,128,1408]{2,1,0:T(8,128)(2,1)S(1)}, bf16[4,640,1280]{2,1,0:T(8,128)(2,1)S(1)}, f32[2,640,256]{2,1,0:T(8,128)S(1)}, bf16[1280,256]{1,0:T(8,128)(2,1)S(1)}) custom-call(s32[1]{0:T(128)} %bitcast.core_ref, bf16[4,640,1280]{2,1,0:T(8,128)(2,1)} %tokens_hbm.1, bf16[1280,256]{1,0:T(8,128)(2,1)} %router_hbm.1), custom_call_target="tpu_custom_call" | custom-call | tf_op jit(solution)/shard_map/pallas_call | solution.py:230
  4.1 1.5 %collective-permute-start = (bf16[2,128,1408]{2,1,0:T(8,128)(2,1)S(1)}, bf16[2,128,1408]{2,1,0:T(8,128)(2,1)S(1)}, u32[]{:S(2)}, u32[]{:S(2)}) collective-permute-start(bf16[2,128,1408]{2,1,0:T(8,128)(2,1)S(1)} %get-tuple-element.18), channel_id=1, source_target_pairs={{0,1},{1,0},{2,3},{3,2},{4,5},{5,4},{6,7},{7,6},{8,9},{9,8},{10,11... | collective-permute-start | bytes 2162696 | tf_op jit(solution)/shard_map/ppermute | solution.py:238
  5.6 0.0 slice-start
  5.7 0.0 slice-start.2
  5.7 1.8 %shard_map.47 = (bf16[2,128,1408]{2,1,0:T(8,128)(2,1)S(1)}, f32[2,640,256]{2,1,0:T(8,128)S(1)}) custom-call(bf16[4,640,1280]{2,1,0:T(8,128)(2,1)S(1)} %get-tuple-element.13.tokens_ref, bf16[1280,256]{1,0:T(8,128)(2,1)S(1)} %get-tuple-element.15.ordered_ref), custom_call_target="tpu_custom_call" | custom-call | tf_op jit(solution)/shard_map/pallas_call | solution.py:240
  7.5 0.1 collective-permute-start.1
  7.6 0.0 slice-start.1
  7.6 0.0 slice-start.3
  7.6 1.7 %shard_map.48 = (bf16[4,128,1408]{2,1,0:T(8,128)(2,1)S(1)}, bf16[4,640,256]{2,1,0:T(8,128)(2,1)S(1)}) custom-call(bf16[4,640,1280]{2,1,0:T(8,128)(2,1)S(1)} %get-tuple-element.13.tokens_ref, f32[2,640,256]{2,1,0:T(8,128)S(1)} %get-tuple-element.14.first_ref, f32[2,640,256]{2,1,0:T(8,128)S(1)} %get-tuple-element.16.last_ref), custom_call_target="tpu_custom_call" | custom-call | tf_op jit(solution)/shard_map/pallas_call | solution.py:249
  9.3 0.0 collective-permute-done.first_ref
  9.4 0.4 collective-permute-done.1.last_ref
  9.8 1.4 %shard_map.49 = bf16[64,8,1408]{2,1,0:T(8,128)(2,1)S(1)} custom-call(bf16[4,128,1408]{2,1,0:T(8,128)(2,1)S(1)} %get-tuple-element.17.mine_ref, bf16[2,128,1408]{2,1,0:T(8,128)(2,1)S(1)} %collective-permute-done.first_ref, bf16[2,128,1408]{2,1,0:T(8,128)(2,1)S(1)} %collective-permute-done.1.last_ref), custom_call_target="tpu_custom_call" | custom-call | tf_op jit(solution)/shard_map/pallas_call | solution.py:260
  11.2 32.3 %all_to_all.10.received_ref = bf16[64,8,1408]{2,1,0:T(8,128)(2,1)S(1)} all-to-all(bf16[64,8,1408]{2,1,0:T(8,128)(2,1)S(1)} %shard_map.49), channel_id=1, replica_groups=mesh['x'=4,'z'=4,'y'=4,'core'=2] {'x','z','y'}, dimensions={0} | all-to-all | bytes 2883584 | tf_op jit(solution)/shard_map/all_to_all | solution.py:268
  43.5 0.0 slice-done
  43.5 0.0 slice-done.2
  43.5 0.0 slice-done.1
  43.5 0.0 slice-done.3
  43.5 2.4 %shard_map.50 = bf16[64,8,1280]{2,1,0:T(8,128)(2,1)S(1)} custom-call(bf16[64,8,1408]{2,1,0:T(8,128)(2,1)S(1)} %all_to_all.10.received_ref, bf16[1,1280,2560]{2,1,0:T(8,128)(2,1)S(1)} %bitcast.2, bf16[1,2560,1280]{2,1,0:T(8,128)(2,1)S(1)} %bitcast.4), custom_call_target="tpu_custom_call" | custom-call | tf_op jit(solution)/shard_map/pallas_call | solution.py:270
  45.9 23.9 %all_to_all.11.ref = bf16[64,8,1280]{2,1,0:T(8,128)(2,1)S(1)} all-to-all(bf16[64,8,1280]{2,1,0:T(8,128)(2,1)S(1)} %shard_map.50), channel_id=1, replica_groups=mesh['x'=4,'z'=4,'y'=4,'core'=2] {'x','z','y'}, dimensions={0} | all-to-all | bytes 2621440 | tf_op jit(solution)/shard_map/all_to_all | solution.py:279
  69.7 4.0 %collective-permute-start.2 = (bf16[64,8,1280]{2,1,0:T(8,128)(2,1)S(1)}, bf16[64,8,1280]{2,1,0:T(8,128)(2,1)S(1)}, u32[]{:S(2)}, u32[]{:S(2)}) collective-permute-start(bf16[64,8,1280]{2,1,0:T(8,128)(2,1)S(1)} %all_to_all.11.ref), channel_id=1, source_target_pairs={{0,1},{1,0},{2,3},{3,2},{4,5},{5,4},{6,7},{7,6},{8,9},{9,8},{10,11... | collective-permute-start | bytes 3932168 | tf_op jit(solution)/shard_map/ppermute | solution.py:280
  73.7 0.5 shard_map.51.mine_ref
  74.2 2.1 %collective-permute-done.2.theirs_ref = bf16[64,8,1280]{2,1,0:T(8,128)(2,1)S(1)} collective-permute-done((bf16[64,8,1280]{2,1,0:T(8,128)(2,1)S(1)}, bf16[64,8,1280]{2,1,0:T(8,128)(2,1)S(1)}, u32[]{:S(2)}, u32[]{:S(2)}) %collective-permute-start.2) | collective-permute-done | bytes 1310752 | tf_op jit(solution)/shard_map/ppermute | solution.py:280
  76.4 3.6 %shard_map.52 = bf16[4,640,1280]{2,1,0:T(8,128)(2,1)} custom-call(bf16[4,128,1280]{2,1,0:T(8,128)(2,1)S(1)} %shard_map.51.mine_ref, bf16[64,8,1280]{2,1,0:T(8,128)(2,1)S(1)} %collective-permute-done.2.theirs_ref, bf16[4,640,256]{2,1,0:T(8,128)(2,1)S(1)} %get-tuple-element.20.combine_ref), custom_call_target="tpu_custom_call" | custom-call | tf_op jit(solution)/shard_map/pallas_call | solution.py:291
  (2 shorter events, 0.0 us)
Async XLA Ops:
  4.1 5.2 %collective-permute-start = (bf16[2,128,1408]{2,1,0:T(8,128)(2,1)S(1)}, bf16[2,128,1408]{2,1,0:T(8,128)(2,1)S(1)}, u32[]{:S(2)}, u32[]{:S(2)}) collective-permute-start(bf16[2,128,1408]{2,1,0:T(8,128)(2,1)S(1)} %get-tuple-element.18), channel_id=1, source_target_pairs={{0,1},{1,0},{2,3},{3,2},{4,5},{5,4},{6,7},{7,6},{8,9},{9,8},{10,11... | collective-permute-start | bytes 2162696 | tf_op jit(solution)/shard_map/ppermute | solution.py:238
  5.6 37.8 %slice-start = ((s8[6553600]{0:T(1024)(128)(4,1)}), s8[4194304]{0:T(1024)(128)(4,1)S(1)}, s32[]{:S(2)}) async-start(s8[6553600]{0:T(1024)(128)(4,1)} %bitcast.1), calls=%async_computation.2 | async-start | bytes 8388608
  5.7 37.8 %slice-start.2 = ((s8[6553600]{0:T(1024)(128)(4,1)}), s8[4194304]{0:T(1024)(128)(4,1)S(1)}, s32[]{:S(2)}) async-start(s8[6553600]{0:T(1024)(128)(4,1)} %bitcast.3), calls=%async_computation.4 | async-start | bytes 8388608
  7.5 2.3 %collective-permute-start.1 = (bf16[2,128,1408]{2,1,0:T(8,128)(2,1)S(1)}, bf16[2,128,1408]{2,1,0:T(8,128)(2,1)S(1)}, u32[]{:S(2)}, u32[]{:S(2)}) collective-permute-start(bf16[2,128,1408]{2,1,0:T(8,128)(2,1)S(1)} %get-tuple-element.19), channel_id=1, source_target_pairs={{0,1},{1,0},{2,3},{3,2},{4,5},{5,4},{6,7},{7,6},{8,9},{9,8},{10,11... | collective-permute-start | bytes 2162696 | tf_op jit(solution)/shard_map/ppermute | solution.py:247
  7.6 35.9 %slice-start.1 = ((s8[6553600]{0:T(1024)(128)(4,1)}), s8[2359296]{0:T(1024)(128)(4,1)S(1)}, s32[]{:S(2)}) async-start(s8[6553600]{0:T(1024)(128)(4,1)} %bitcast.1), calls=%async_computation.3 | async-start | bytes 4718592
  7.6 35.9 %slice-start.3 = ((s8[6553600]{0:T(1024)(128)(4,1)}), s8[2359296]{0:T(1024)(128)(4,1)S(1)}, s32[]{:S(2)}) async-start(s8[6553600]{0:T(1024)(128)(4,1)} %bitcast.3), calls=%async_computation.5 | async-start | bytes 4718592
  69.7 6.6 %collective-permute-start.2 = (bf16[64,8,1280]{2,1,0:T(8,128)(2,1)S(1)}, bf16[64,8,1280]{2,1,0:T(8,128)(2,1)S(1)}, u32[]{:S(2)}, u32[]{:S(2)}) collective-permute-start(bf16[64,8,1280]{2,1,0:T(8,128)(2,1)S(1)} %all_to_all.11.ref), channel_id=1, source_target_pairs={{0,1},{1,0},{2,3},{3,2},{4,5},{5,4},{6,7},{7,6},{8,9},{9,8},{10,11... | collective-permute-start | bytes 3932168 | tf_op jit(solution)/shard_map/ppermute | solution.py:280

commit v7 on v5

--- a/solution.py
+++ b/solution.py
@@ -177,8 +177,7 @@
             out_ref[:, group * part:group * part + part, lo:lo + 256] = moved.reshape(clips, part, 256)
 
 
-def window_kernel(mine_ref, first_ref, last_ref, slots_ref, combine_ref):
-    by_clip(mine_ref, slots_ref)
+def combine_kernel(first_ref, last_ref, combine_ref):
     now = first_ref.shape[0]
     for c in range(combine_ref.shape[0]):
         logits = first_ref[c] if c < now else last_ref[c - now]
@@ -271,6 +270,15 @@
 
     received = lax.all_to_all(merged, chips, 0, 0, tiled=False)
 
+    combine = pl.pallas_call(
+        combine_kernel,
+        in_specs=[whole] * 2,
+        out_specs=whole,
+        out_shape=jax.ShapeDtypeStruct((clips, count, slots), BF16),
+        compiler_params=params(16),
+        cost_estimate=pl.CostEstimate(flops=4 * 10**6, bytes_accessed=4 * 10**6, transcendentals=7 * 10**5),
+    )(first_logits, last_logits)
+
     results = pl.pallas_call(
         functools.partial(expert_kernel, 256),
         in_specs=[whole] * 3,
@@ -283,16 +291,13 @@
     returned = lax.all_to_all(results, chips, 0, 0, tiled=False)
     partner = lax.ppermute(returned, "core", swap)
 
-    own, combine = pl.pallas_call(
-        window_kernel,
-        in_specs=[whole] * 3,
-        out_specs=[whole] * 2,
-        out_shape=[
-            jax.ShapeDtypeStruct((clips, half, depth), BF16),
-            jax.ShapeDtypeStruct((clips, count, slots), BF16),
-        ],
-        compiler_params=params(16),
-    )(returned, first_logits, last_logits)
+    own = pl.pallas_call(
+        by_clip,
+        in_specs=[whole],
+        out_specs=whole,
+        out_shape=jax.ShapeDtypeStruct((clips, half, depth), BF16),
+        compiler_params=params(16),
+    )(returned)
 
     tile = count // 4
     return pl.pallas_call(

time: 80.2 us -> 80.2 us (level)
  transfers between devices with their start and end apart: 3 -> 3, of which waited for: 2 -> 2; matrix products, arithmetic and copies ran while one was open for 0% -> 0% of each run, Pallas kernels for 5% -> 6%
where the time goes in v7:
time: 80.2 us; the launch traced here: 80.1 us
  blocking collectives  56.2 us (70%)
  Pallas kernels  16.1 us (20%)
  starting transfers between devices  5.58 us (7%)
  waiting for transfers between devices  1.98 us (2%)
    all_to_all x1, blocking collectives, shards(): received = lax.all_to_all(merged, chips, 0, 0, tiled=False)  32.3 us
    all_to_all x1, blocking collectives, shards(): returned = lax.all_to_all(results, chips, 0, 0, tiled=False)  23.9 us
    pallas_call x1, Pallas kernels, shards(): pl.pallas_call(first_scores_kernel, in_specs=[pl.BlockSpec(memory_space=p...  4.15 us
    ppermute x1, starting transfers between devices, shards(): partner = lax.ppermute(returned, 'core', swap)  3.96 us
    pallas_call x1, Pallas kernels, shards(): pl.pallas_call(functools.partial(mix_kernel, tile), in_specs=[whole] * 3,...  3.51 us
    pallas_call x1, Pallas kernels, shards(): pl.pallas_call(functools.partial(expert_kernel, 256), in_specs=[whole] *...  2.35 us
    pallas_call x1, Pallas kernels, shards(): pl.pallas_call(last_scores_kernel, in_specs=[whole] * 2, out_specs=[whole...  1.84 us
  transfers between devices with their start and end apart: 3, of which 2 were waited for; matrix products, arithmetic and copies ran while one was open for 0% of the time, Pallas kernels for 6%

profile of v7, /device:TPU:1, one launch (start us, length us, event | category | flops | bytes accessed | tf_op | source)
XLA Modules:
  0.0 80.1 jit_solution(17978728011247153161)
XLA Ops:
  0.0 4.1 %shard_map.46 = (bf16[2,128,1408]{2,1,0:T(8,128)(2,1)S(1)}, bf16[4,640,1280]{2,1,0:T(8,128)(2,1)S(1)}, f32[2,640,256]{2,1,0:T(8,128)S(1)}, bf16[1280,256]{1,0:T(8,128)(2,1)S(1)}) custom-call(s32[1]{0:T(128)} %bitcast.core_ref, bf16[4,640,1280]{2,1,0:T(8,128)(2,1)} %tokens_hbm.1, bf16[1280,256]{1,0:T(8,128)(2,1)} %router_hbm.1), custom_call_target="tpu_custom_call" | custom-call | tf_op jit(solution)/shard_map/pallas_call | solution.py:236
  4.2 1.5 %collective-permute-start = (bf16[2,128,1408]{2,1,0:T(8,128)(2,1)S(1)}, bf16[2,128,1408]{2,1,0:T(8,128)(2,1)S(1)}, u32[]{:S(2)}, u32[]{:S(2)}) collective-permute-start(bf16[2,128,1408]{2,1,0:T(8,128)(2,1)S(1)} %get-tuple-element.15), channel_id=1, source_target_pairs={{0,1},{1,0},{2,3},{3,2},{4,5},{5,4},{6,7},{7,6},{8,9},{9,8},{10,11... | collective-permute-start | bytes 2162696 | tf_op jit(solution)/shard_map/ppermute | solution.py:244
  5.7 0.0 slice-start
  5.7 0.0 slice-start.2
  5.7 1.8 %shard_map.47 = (bf16[2,128,1408]{2,1,0:T(8,128)(2,1)S(1)}, f32[2,640,256]{2,1,0:T(8,128)S(1)}) custom-call(bf16[4,640,1280]{2,1,0:T(8,128)(2,1)S(1)} %get-tuple-element.11.tokens_ref, bf16[1280,256]{1,0:T(8,128)(2,1)S(1)} %get-tuple-element.13.ordered_ref), custom_call_target="tpu_custom_call" | custom-call | tf_op jit(solution)/shard_map/pallas_call | solution.py:246
  7.5 0.1 collective-permute-start.1
  7.6 0.0 slice-start.1
  7.6 0.0 slice-start.3
  7.6 1.5 %shard_map.48.mine_ref = bf16[4,128,1408]{2,1,0:T(8,128)(2,1)S(1)} custom-call(bf16[4,640,1280]{2,1,0:T(8,128)(2,1)S(1)} %get-tuple-element.11.tokens_ref, f32[2,640,256]{2,1,0:T(8,128)S(1)} %get-tuple-element.12.first_ref, f32[2,640,256]{2,1,0:T(8,128)S(1)} %get-tuple-element.14.last_ref), custom_call_target="tpu_custom_call" | custom-call | tf_op jit(solution)/shard_map/pallas_call | solution.py:255
  9.2 0.0 collective-permute-done.first_ref
  9.2 0.6 collective-permute-done.1.last_ref
  9.8 1.4 %shard_map.49 = bf16[64,8,1408]{2,1,0:T(8,128)(2,1)S(1)} custom-call(bf16[4,128,1408]{2,1,0:T(8,128)(2,1)S(1)} %shard_map.48.mine_ref, bf16[2,128,1408]{2,1,0:T(8,128)(2,1)S(1)} %collective-permute-done.first_ref, bf16[2,128,1408]{2,1,0:T(8,128)(2,1)S(1)} %collective-permute-done.1.last_ref), custom_call_target="tpu_custom_call" | custom-call | tf_op jit(solution)/shard_map/pallas_call | solution.py:263
  11.2 32.3 %all_to_all.10.received_ref = bf16[64,8,1408]{2,1,0:T(8,128)(2,1)S(1)} all-to-all(bf16[64,8,1408]{2,1,0:T(8,128)(2,1)S(1)} %shard_map.49), channel_id=1, replica_groups=mesh['x'=4,'z'=4,'y'=4,'core'=2] {'x','z','y'}, dimensions={0} | all-to-all | bytes 2883584 | tf_op jit(solution)/shard_map/all_to_all | solution.py:271
  43.5 0.0 slice-done
  43.5 0.0 slice-done.2
  43.5 0.0 slice-done.1
  43.5 0.0 slice-done.3
  43.6 2.4 %shard_map.50 = bf16[64,8,1280]{2,1,0:T(8,128)(2,1)S(1)} custom-call(bf16[64,8,1408]{2,1,0:T(8,128)(2,1)S(1)} %all_to_all.10.received_ref, bf16[1,1280,2560]{2,1,0:T(8,128)(2,1)S(1)} %bitcast.2, bf16[1,2560,1280]{2,1,0:T(8,128)(2,1)S(1)} %bitcast.4), custom_call_target="tpu_custom_call" | custom-call | tf_op jit(solution)/shard_map/pallas_call | solution.py:282
  45.9 23.9 %all_to_all.11.ref = bf16[64,8,1280]{2,1,0:T(8,128)(2,1)S(1)} all-to-all(bf16[64,8,1280]{2,1,0:T(8,128)(2,1)S(1)} %shard_map.50), channel_id=1, replica_groups=mesh['x'=4,'z'=4,'y'=4,'core'=2] {'x','z','y'}, dimensions={0} | all-to-all | bytes 2621440 | tf_op jit(solution)/shard_map/all_to_all | solution.py:291
  69.8 4.0 %collective-permute-start.2 = (bf16[64,8,1280]{2,1,0:T(8,128)(2,1)S(1)}, bf16[64,8,1280]{2,1,0:T(8,128)(2,1)S(1)}, u32[]{:S(2)}, u32[]{:S(2)}) collective-permute-start(bf16[64,8,1280]{2,1,0:T(8,128)(2,1)S(1)} %all_to_all.11.ref), channel_id=1, source_target_pairs={{0,1},{1,0},{2,3},{3,2},{4,5},{5,4},{6,7},{7,6},{8,9},{9,8},{10,11... | collective-permute-start | bytes 3932168 | tf_op jit(solution)/shard_map/ppermute | solution.py:292
  73.7 0.8 shard_map.52.combine_ref
  74.5 0.5 shard_map.51.mine_ref
  75.0 1.4 %collective-permute-done.2.theirs_ref = bf16[64,8,1280]{2,1,0:T(8,128)(2,1)S(1)} collective-permute-done((bf16[64,8,1280]{2,1,0:T(8,128)(2,1)S(1)}, bf16[64,8,1280]{2,1,0:T(8,128)(2,1)S(1)}, u32[]{:S(2)}, u32[]{:S(2)}) %collective-permute-start.2) | collective-permute-done | bytes 1310752 | tf_op jit(solution)/shard_map/ppermute | solution.py:292
  76.4 3.5 %shard_map.53 = bf16[4,640,1280]{2,1,0:T(8,128)(2,1)} custom-call(bf16[4,128,1280]{2,1,0:T(8,128)(2,1)S(1)} %shard_map.51.mine_ref, bf16[64,8,1280]{2,1,0:T(8,128)(2,1)S(1)} %collective-permute-done.2.theirs_ref, bf16[4,640,256]{2,1,0:T(8,128)(2,1)S(1)} %shard_map.52.combine_ref), custom_call_target="tpu_custom_call" | custom-call | tf_op jit(solution)/shard_map/pallas_call | solution.py:303
  (2 shorter events, 0.0 us)
Async XLA Ops:
  4.2 5.0 %collective-permute-start = (bf16[2,128,1408]{2,1,0:T(8,128)(2,1)S(1)}, bf16[2,128,1408]{2,1,0:T(8,128)(2,1)S(1)}, u32[]{:S(2)}, u32[]{:S(2)}) collective-permute-start(bf16[2,128,1408]{2,1,0:T(8,128)(2,1)S(1)} %get-tuple-element.15), channel_id=1, source_target_pairs={{0,1},{1,0},{2,3},{3,2},{4,5},{5,4},{6,7},{7,6},{8,9},{9,8},{10,11... | collective-permute-start | bytes 2162696 | tf_op jit(solution)/shard_map/ppermute | solution.py:244
  5.7 37.9 %slice-start = ((s8[6553600]{0:T(1024)(128)(4,1)}), s8[4194304]{0:T(1024)(128)(4,1)S(1)}, s32[]{:S(2)}) async-start(s8[6553600]{0:T(1024)(128)(4,1)} %bitcast.1), calls=%async_computation.2 | async-start | bytes 8388608
  5.7 37.9 %slice-start.2 = ((s8[6553600]{0:T(1024)(128)(4,1)}), s8[4194304]{0:T(1024)(128)(4,1)S(1)}, s32[]{:S(2)}) async-start(s8[6553600]{0:T(1024)(128)(4,1)} %bitcast.3), calls=%async_computation.4 | async-start | bytes 8388608
  7.5 2.3 %collective-permute-start.1 = (bf16[2,128,1408]{2,1,0:T(8,128)(2,1)S(1)}, bf16[2,128,1408]{2,1,0:T(8,128)(2,1)S(1)}, u32[]{:S(2)}, u32[]{:S(2)}) collective-permute-start(bf16[2,128,1408]{2,1,0:T(8,128)(2,1)S(1)} %get-tuple-element.16), channel_id=1, source_target_pairs={{0,1},{1,0},{2,3},{3,2},{4,5},{5,4},{6,7},{7,6},{8,9},{9,8},{10,11... | collective-permute-start | bytes 2162696 | tf_op jit(solution)/shard_map/ppermute | solution.py:253
  7.6 35.9 %slice-start.1 = ((s8[6553600]{0:T(1024)(128)(4,1)}), s8[2359296]{0:T(1024)(128)(4,1)S(1)}, s32[]{:S(2)}) async-start(s8[6553600]{0:T(1024)(128)(4,1)} %bitcast.1), calls=%async_computation.3 | async-start | bytes 4718592
  7.6 35.9 %slice-start.3 = ((s8[6553600]{0:T(1024)(128)(4,1)}), s8[2359296]{0:T(1024)(128)(4,1)S(1)}, s32[]{:S(2)}) async-start(s8[6553600]{0:T(1024)(128)(4,1)} %bitcast.3), calls=%async_computation.5 | async-start | bytes 4718592
  69.8 6.6 %collective-permute-start.2 = (bf16[64,8,1280]{2,1,0:T(8,128)(2,1)S(1)}, bf16[64,8,1280]{2,1,0:T(8,128)(2,1)S(1)}, u32[]{:S(2)}, u32[]{:S(2)}) collective-permute-start(bf16[64,8,1280]{2,1,0:T(8,128)(2,1)S(1)} %all_to_all.11.ref), channel_id=1, source_target_pairs={{0,1},{1,0},{2,3},{3,2},{4,5},{5,4},{6,7},{7,6},{8,9},{9,8},{10,11... | collective-permute-start | bytes 3932168 | tf_op jit(solution)/shard_map/ppermute | solution.py:292
